TPU v7x, 128 devices: a whole 4x4x4 slice. The times are simulated.
128 devices in a mesh: pipe: 8 (over x, core), expert: 16 (over z, y).
Axes of the slice: x: 4, y: 4, z: 4, core: 2. Of those that a mesh axis runs over, the one named last changes fastest.
Arguments:
- tokens: bfloat16 [16384, 7168], P(('pipe', 'expert')), may hold values from -6 to 6
- cotangent: bfloat16 [16384, 7168], P(('pipe', 'expert')), may hold values from -6 to 6
- expert_ids: int32 [16384, 8], P(('pipe', 'expert')), may hold values from 0 to 255, as said below
- gate_probs: bfloat16 [16384, 8], P(('pipe', 'expert')), may hold values from 0.049804688 to 1
- w_gate: bfloat16 [16, 7168, 2048], P('expert', None, 'pipe'), may hold values from -0.0625 to 0.0625
- w_up: bfloat16 [16, 7168, 2048], P('expert', None, 'pipe'), may hold values from -0.0625 to 0.0625
- w_down: bfloat16 [16, 2048, 7168], P('expert', 'pipe'), may hold values from -0.125 to 0.125
Outputs:
- grad_gate_w: bfloat16 [16, 7168, 2048], P('expert', None, 'pipe')
- grad_up_w: bfloat16 [16, 7168, 2048], P('expert', None, 'pipe')
- grad_down_w: bfloat16 [16, 2048, 7168], P('expert', 'pipe')
- gate_grad: float32 [16384, 8], P(('pipe', 'expert'))
Inputs may be any that keep to these rules, and one draw needn't show every extreme that they name: `expert_ids`: each token's 8 ids are distinct and its k-th id lies in group k, that is among k * 32 to (k + 1) * 32 - 1. The tokens of one device (aligned blocks of 128 rows) name any expert of the window at most 8 times, and one expert of the window is named exactly 8 times in every block.
All inputs are finite; a program needn't handle non-finite values.
Results may differ from a plain program's by a relative error of at most 0.011.
Values may be sent and summed in bfloat16 or wider, within the bound.
No kernel may reach another device: no remote copies, remote signals or barrier semaphores. Data moves between devices by JAX's collectives and lax.ppermute only.
A program may use at most 192 MiB of HBM per device.

v0:
```python
import math

import jax
import jax.numpy as jnp
from jax import lax
from jax.experimental import pallas as pl
from jax.experimental.pallas import tpu as pltpu
from jax.sharding import Mesh, PartitionSpec as P

GROUPS = 8
CAP = 8
GROUP_SIZE = 32
NX, NC, NZ, NY = 4, 2, 4, 4

X_RAW, X_REST = 1792, 5376
BLOCK, END_BLOCK = 1792, 896
PARAMS = pltpu.CompilerParams(vmem_limit_bytes=62 * 2**20)


def after(x, *others):
    return x if not others else lax.optimization_barrier((x, *others))[0]


def shift(x, axis, by):
    n = lax.axis_size(axis)
    return lax.ppermute(x, axis, [(i, (i + by) % n) for i in range(n)])


def exchange_yz(tiles):
    return lax.all_to_all(tiles, ("z", "y"), 0, 0, tiled=True).reshape(-1, tiles.shape[2])


def hop(x, by):
    pairs = [(i * NC + c, (i + by * (1 - 2 * c)) % NX * NC + c) for i in range(NX) for c in range(NC)]
    return lax.ppermute(x, ("x", "core"), pairs)


SMALL = pl.CostEstimate(flops=1, bytes_accessed=1, transcendentals=0)
ANY = pl.BlockSpec(memory_space=pl.ANY)


def whole_parts(parts):
    return [part if isinstance(part, tuple) else (part, 0, part.shape[1]) for part in parts]


def row_specs(parts, block, step=lambda i: i):
    return [
        pl.BlockSpec((part.shape[0], block), lambda i, first=at // block: (0, first + step(i))) for part, at, _ in parts
    ]


def joined(refs):
    return jnp.concatenate([ref[...] for ref in refs])


def forward(parts, w_gate, w_up, at, all_rows, row=0, pre=None):
    parts = whole_parts(parts)
    size, count = parts[0][2], len(parts)
    rows = sum(part.shape[0] for part, _, _ in parts)
    width = w_gate.shape[2]
    block = math.gcd(BLOCK, size, at)
    first = at // block

    def kernel(*refs):
        out_ref = refs[-1]

        @pl.when(pl.program_id(0) == 0)
        def _():
            out_ref[...] = jnp.zeros_like(out_ref)

        x = joined(refs[2 : 2 + count])
        for j, w_ref in enumerate(refs[:2]):
            out_ref[:, j * width : (j + 1) * width] += jnp.dot(x, w_ref[0], preferred_element_type=jnp.float32)

    return pl.pallas_call(
        kernel,
        grid=(size // block,),
        in_specs=[pl.BlockSpec((1, block, width), lambda i: (0, first + i, 0))] * 2
        + row_specs(parts, block)
        + ([] if pre is None else [ANY]),
        out_specs=pl.BlockSpec((rows, 2 * width), lambda i: (row // rows, 0)),
        out_shape=jax.ShapeDtypeStruct((all_rows, 2 * width), jnp.float32),
        input_output_aliases={} if pre is None else {2 + count: 0},
        compiler_params=PARAMS,
        cost_estimate=SMALL,
    )(w_gate, w_up, *[part[0] for part in parts], *(() if pre is None else (pre,)))


def forward_end(parts, w_gate, w_up, at, pre):
    parts = whole_parts(parts)
    size, count = parts[0][2], len(parts)
    rows = pre.shape[0]
    width = w_gate.shape[2]
    block = math.gcd(END_BLOCK, size, at)
    first, steps = at // block, size // block
    strip = 128

    def kernel(*refs):
        pre_ref = refs[2 + count]
        activated_ref, slope_ref, hidden_ref, turned_ref, total = refs[-5:]

        @pl.when(pl.program_id(0) == 0)
        def _():
            total[...] = pre_ref[...]

        x = joined(refs[2 : 2 + count])
        for j, w_ref in enumerate(refs[:2]):
            total[:, j * width : (j + 1) * width] += jnp.dot(x, w_ref[0], preferred_element_type=jnp.float32)

        @pl.when(pl.program_id(0) == steps - 1)
        def _():
            for k in range(0, rows, strip):
                place = slice(k, k + strip)
                pre_gate, pre_up = total[place, :width], total[place, width:]
                sig = jax.nn.sigmoid(pre_gate)
                activated = pre_gate * sig
                hidden = (activated * pre_up).astype(jnp.bfloat16)
                activated_ref[place] = activated
                slope_ref[place] = pre_up * sig * (1.0 + pre_gate * (1.0 - sig))
                hidden_ref[place] = hidden
                turned_ref[:, place] = hidden.T

    def whole(*shape):
        return pl.BlockSpec(shape, lambda i: (0, 0))

    flat = jax.ShapeDtypeStruct((rows, width), jnp.float32)
    return pl.pallas_call(
        kernel,
        grid=(steps,),
        in_specs=[pl.BlockSpec((1, block, width), lambda i: (0, first + i, 0))] * 2
        + row_specs(parts, block)
        + [whole(*pre.shape)],
        out_specs=[whole(rows, width)] * 3 + [whole(width, rows)],
        out_shape=[
            flat,
            flat,
            jax.ShapeDtypeStruct((rows, width), jnp.bfloat16),
            jax.ShapeDtypeStruct((width, rows), jnp.bfloat16),
        ],
        scratch_shapes=[pltpu.VMEM(pre.shape, jnp.float32)],
        compiler_params=PARAMS,
        cost_estimate=SMALL,
    )(w_gate, w_up, *[part[0] for part in parts], pre)


def down_terms(parts, w_down, turned, activated, slope, hidden, order):
    parts = whole_parts(parts)
    size, count = parts[0][2], len(parts)
    rows, width = hidden.shape
    block = math.gcd(BLOCK, size)
    steps = size // block
    strip = rows // (NX * NC)

    def kernel(*refs):
        order_ref, down_ref, turned_ref = refs[:3]
        late_refs = refs[3:6]
        grad_ref, gate_ref, up_ref, row_ref, projected_ref = refs[-9:-4]
        held, sems = refs[-4:-1], refs[-1]
        copies = [pltpu.make_async_copy(late, own, sems.at[k]) for k, (late, own) in enumerate(zip(late_refs, held))]

        @pl.when(pl.program_id(0) == 0)
        def _():
            for copy in copies:
                copy.start()
            projected_ref[...] = jnp.zeros_like(projected_ref)

        dy = joined(refs[6 : 6 + count])
        projected_ref[...] += lax.dot_general(
            dy, down_ref[0], (((1,), (1,)), ((), ())), preferred_element_type=jnp.float32
        )
        grad_ref[0] = jnp.dot(turned_ref[...], dy, preferred_element_type=jnp.float32).astype(jnp.bfloat16)

        @pl.when(pl.program_id(0) == steps - 1)
        def _():
            for copy in copies:
                copy.wait()
            activated_ref, slope_ref, hidden_ref = held

            def some(k, _):
                at_rows = pl.ds(pl.multiple_of(k * strip, strip), strip)
                projected = projected_ref[at_rows]
                gate_ref[at_rows] = (projected * slope_ref[at_rows]).astype(jnp.bfloat16)
                up_ref[at_rows] = (projected * activated_ref[at_rows]).astype(jnp.bfloat16)
                sums = jnp.sum(hidden_ref[at_rows].astype(jnp.float32) * projected, axis=1, keepdims=True)
                row_ref[pl.ds(order_ref[k], 1)] = jnp.broadcast_to(sums, (strip, strip)).T[:1]
                return 0

            lax.fori_loop(0, rows // strip, some, 0)

    def whole(*shape):
        return pl.BlockSpec(shape, lambda i: (0, 0))

    wide = pl.BlockSpec((1, width, block), lambda i: (0, 0, i))
    grad = jax.ShapeDtypeStruct((rows, width), jnp.bfloat16)
    late = (activated, slope, hidden)
    return pl.pallas_call(
        kernel,
        grid=(steps,),
        in_specs=[pl.BlockSpec(memory_space=pltpu.SMEM), wide, whole(width, rows)]
        + [ANY] * len(late)
        + row_specs(parts, block),
        out_specs=[wide, whole(rows, width), whole(rows, width), whole(NX * NC, strip)],
        out_shape=[
            jax.ShapeDtypeStruct(w_down.shape, jnp.bfloat16),
            grad,
            grad,
            jax.ShapeDtypeStruct((NX * NC, strip), jnp.float32),
        ],
        scratch_shapes=[pltpu.VMEM((rows, width), jnp.float32)]
        + [pltpu.VMEM(a.shape, a.dtype) for a in late]
        + [pltpu.SemaphoreType.DMA((len(late),))],
        compiler_params=PARAMS,
        cost_estimate=SMALL,
    )(order, w_down, turned, *late, *[part[0] for part in parts])


def up_terms(parts, last_parts, grad_pre_gate, grad_pre_up):
    rows, width = grad_pre_gate.shape
    parts, last_parts = whole_parts(parts), whole_parts(last_parts)
    count, size, last = len(parts), parts[0][2], last_parts[0][2]
    block = math.gcd(BLOCK, size, last)
    steps, last_steps = size // block, last // block

    def kernel(*refs):
        out_refs = refs[-2:]

        def write(row_refs):
            x = joined(row_refs)
            for pre_ref, out_ref in zip(refs[:2], out_refs):
                out_ref[0] = lax.dot_general(
                    x, pre_ref[...], (((0,), (0,)), ((), ())), preferred_element_type=jnp.float32
                ).astype(jnp.bfloat16)

        pl.when(pl.program_id(0) < steps)(lambda: write(refs[2 : 2 + count]))
        pl.when(pl.program_id(0) >= steps)(lambda: write(refs[2 + count : -2]))

    out = jax.ShapeDtypeStruct((1, size + last, width), jnp.bfloat16)
    whole = pl.BlockSpec((rows, width), lambda i: (0, 0))
    return pl.pallas_call(
        kernel,
        grid=(steps + last_steps,),
        in_specs=[whole, whole]
        + row_specs(parts, block, lambda i: jnp.minimum(i, steps - 1))
        + row_specs(last_parts, block, lambda i: jnp.maximum(i - steps, 0)),
        out_specs=[pl.BlockSpec((1, block, width), lambda i: (0, i, 0))] * 2,
        out_shape=[out, out],
        compiler_params=PARAMS,
        cost_estimate=SMALL,
    )(grad_pre_gate, grad_pre_up, *[part[0] for part in (*parts, *last_parts)])


def row_order():
    x, core = lax.axis_index("x"), lax.axis_index("core")
    near = [(c, by) for c in (core, 1 - core) for by in (0, 1, -1)]
    return jnp.stack([(x - by * (1 - 2 * c)) % NX * NC + c for c, by in near + [(core, 2), (1 - core, 2)]]).astype(jnp.int32)


def return_rows(row_gate):
    got = lax.all_to_all(row_gate.reshape(-1, CAP), ("x", "core", "z", "y"), 0, 0, tiled=True)
    return jnp.sum(got.reshape(NC * NX, NZ * NY, CAP), axis=0)


def per_device(tokens, cotangent, expert_ids, gate_probs, w_gate, w_up, w_down):
    tok_here = tokens.shape[0]
    columns = NZ * NY
    experts = jnp.arange(columns, dtype=jnp.int32)
    routed = experts % GROUPS * GROUP_SIZE + experts // GROUPS
    matches = expert_ids[:, :, None] == routed[None, None, :]
    routed_here = jnp.any(matches, axis=1).astype(jnp.int32)
    slot_rank = jnp.cumsum(routed_here, axis=0) - routed_here
    slot_hot = jnp.logical_and(
        slot_rank[:, :, None] == jnp.arange(CAP, dtype=jnp.int32)[None, None, :],
        routed_here[:, :, None] == 1,
    )
    gates = gate_probs.astype(jnp.float32)
    gate_sel = jnp.sum(jnp.where(matches, gates[:, :, None], 0.0), axis=1)
    placer = slot_hot.astype(jnp.bfloat16).reshape(tok_here, columns * CAP)
    placer_gate = (
        jnp.where(slot_hot, gate_sel[:, :, None], 0.0).astype(jnp.bfloat16).reshape(tok_here, columns * CAP)
    )
    width = w_gate.shape[2]

    def tiles_of(place, source, at, size):
        tiles = lax.dot_general(
            place, source[:, at : at + size], (((0,), (0,)), ((), ())), preferred_element_type=jnp.float32
        )
        return tiles.astype(jnp.bfloat16).reshape(columns, CAP, size)

    def on(block, *ties):
        return hop(after(block, *ties), 1)

    def back(block, *ties):
        return hop(after(block, *ties), -1)

    def swap(part):
        return shift(part, "core", 1)

    features = tokens.shape[1]
    all_rows = NX * NC * columns * CAP
    split = all_rows * 3 // 4

    raw = tiles_of(placer, tokens, X_REST, X_RAW).reshape(-1, X_RAW)
    on_r, back_r = hop(raw, 1), hop(raw, -1)
    x = exchange_yz(after(tiles_of(placer, tokens, 0, X_REST), raw))
    rounds = [part.reshape(columns, CAP, X_RAW) for part in (raw, on_r, back_r, hop(on_r, 1))]
    dy = tiles_of(placer_gate, cotangent, 0, features)
    rounds = jnp.concatenate(rounds, axis=2)

    ties = (x, rounds, dy, row_order())
    order = lax.optimization_barrier(ties)[3]
    on_x, back_x = on(x, *ties), back(x, *ties)
    other_x = swap(after(x, *ties))
    dy = exchange_yz(after(dy, *ties))

    ties = (dy, on_x, back_x, other_x)
    again_x, on_dy, back_dy = on(on_x, *ties), on(dy, *ties), back(dy, *ties)
    rounds = exchange_yz(after(rounds, *ties))
    near_x = lax.optimization_barrier((x, on_x, back_x, *ties))[:3]
    near_x = (*near_x, other_x, swap(near_x[1]), swap(near_x[2]))
    other_dy = swap(after(dy, *ties))
    pre = forward(near_x, w_gate, w_up, 0, all_rows)

    ties = (rounds, again_x, on_dy, back_dy, other_dy, pre)
    again_dy = on(on_dy, *ties)
    again_x = (after(again_x, *ties), swap(after(again_x, *ties)))
    rounds = after(rounds, *ties)
    rounds = (rounds, swap(rounds))
    raw_rows = [(part, k * X_RAW, X_RAW) for ks in ((0, 1, 2), (3,)) for part in rounds for k in ks]
    near_dy = lax.optimization_barrier((dy, on_dy, back_dy, *ties))[:3]
    near_dy = (*near_dy, other_dy, swap(near_dy[1]), swap(near_dy[2]))
    pre = forward(again_x, w_gate, w_up, 0, all_rows, split, pre)
    activated, slope, hidden, turned = forward_end(raw_rows, w_gate, w_up, X_REST, pre)

    ties = (again_dy, *near_dy, turned)
    again_dy = (again_dy, swap(after(again_dy, *ties)))
    grad_down, grad_pre_gate, grad_pre_up, row_gate = down_terms(
        (*near_dy, *again_dy), w_down, turned, activated, slope, hidden, order
    )
    returned = return_rows(row_gate).reshape(columns, CAP)
    grads = up_terms((*near_x, *again_x), raw_rows, grad_pre_gate, grad_pre_up)

    slot_values = jnp.sum(jnp.where(slot_hot, returned[None], 0.0), axis=2)
    picked = jnp.sum(jnp.where(matches, slot_values[:, None, :], 0.0), axis=2)
    gate_grad = picked / gates
    return *grads, grad_down, gate_grad


def solution(mesh):
    mesh = Mesh(mesh.devices.reshape(NX, NC, NZ, NY), ("x", "core", "z", "y"))
    tokens = P(("x", "core", "z", "y"), None)
    wide = P(("z", "y"), None, ("x", "core"))
    deep = P(("z", "y"), ("x", "core"), None)
    return jax.shard_map(
        per_device,
        mesh=mesh,
        in_specs=(tokens, tokens, tokens, tokens, wide, wide, deep),
        out_specs=(wide, wide, deep, tokens),
        check_vma=False,
    )
```

profile of v0, /device:TPU:1, one launch (start us, length us, event | category | flops | bytes accessed | tf_op | source)
XLA Modules:
  0.0 209.3 jit_solution(3747812756165771461)
XLA Ops:
  0.7 0.1 eq.66
  0.8 0.9 compare_reduce_fusion
  1.6 0.1 copy.24
  1.9 0.2 reduce_window_sum.11
  2.1 2.1 %convolution_convert_fusion.2 = bf16[128,1792]{1,0:T(8,128)(2,1)} fusion(bf16[128,7168]{1,0:T(8,128)(2,1)} %param.7, s32[128]{0:T(128)S(1)} %eq.66, s32[128,16]{0,1:T(8,128)S(1)} %copy.25, pred[128,16]{0,1:T(8,128)(4,1)S(1)} %copy.26), kind=kOutput, calls=%fused_computation.4 | convolution fusion | flops 58982400 | bytes 928256 | tf_op jit(solution)/shard_map/dot_general | solution.py:284
  4.2 3.3 %collective-permute-start = (bf16[128,1792]{1,0:T(8,128)(2,1)}, bf16[128,1792]{1,0:T(8,128)(2,1)}, u32[]{:S(2)}, u32[]{:S(2)}) collective-permute-start(bf16[128,1792]{1,0:T(8,128)(2,1)} %convolution_convert_fusion.2), channel_id=1, source_target_pairs={{0,32},{16,112},{32,64},{48,16},{64,96},{80,48},{96,0},{112,80},{1... | collective-permute-start | bytes 1376264 | tf_op jit(solution)/shard_map/ppermute | solution.py:35
  7.6 3.0 %fusion.1 = bf16[16,8,5376]{2,1,0:T(8,128)(2,1)} fusion(bf16[128,7168]{1,0:T(8,128)(2,1)} %param.7, s32[128]{0:T(128)S(1)} %eq.66, s32[128,16]{0,1:T(8,128)S(1)} %copy.25, pred[128,16]{0,1:T(8,128)(4,1)S(1)} %copy.26), kind=kOutput, calls=%fused_computation.3 | convolution fusion | flops 176881664 | bytes 2763264 | tf_op jit(solution)/shard_map/dot_general | solution.py:284
  10.5 7.9 %all-to-all-start = ((bf16[16,8,5376]{2,1,0:T(8,128)(2,1)}), bf16[16,8,5376]{2,1,0:T(8,128)(2,1)S(1)}, u32[]{:S(2)}, u32[]{:S(2)}) async-start(bf16[16,8,5376]{2,1,0:T(8,128)(2,1)} %fusion.1), calls=%async_computation | async-start | bytes 2752512 | tf_op jit(solution)/shard_map/all_to_all | solution.py:30
  18.4 0.1 collective-permute-start.1
  18.5 2.7 %collective-permute-start.2 = (bf16[128,1792]{1,0:T(8,128)(2,1)}, bf16[128,1792]{1,0:T(8,128)(2,1)}, u32[]{:S(2)}, u32[]{:S(2)}) collective-permute-start(bf16[128,1792]{1,0:T(8,128)(2,1)} %collective-permute-done), channel_id=1, source_target_pairs={{0,32},{16,112},{32,64},{48,16},{64,96},{80,48},{96,0},{112,80},{1... | collective-permute-start | bytes 1376264 | tf_op jit(solution)/shard_map/ppermute | solution.py:35
  21.2 0.6 stack.35.refs_0_
  21.8 0.1 fusion.4
  21.9 1.9 fusion
  23.8 6.5 %collective-permute-done.1 = bf16[128,1792]{1,0:T(8,128)(2,1)} collective-permute-done((bf16[128,1792]{1,0:T(8,128)(2,1)}, bf16[128,1792]{1,0:T(8,128)(2,1)}, u32[]{:S(2)}, u32[]{:S(2)}) %collective-permute-start.1) | collective-permute-done | bytes 458784 | tf_op jit(solution)/shard_map/ppermute | solution.py:35
  30.3 0.8 collective-permute-done.2
  31.1 2.8 %pad_maximum_fusion = bf16[16,8,7168]{2,1,0:T(8,128)(2,1)} fusion(bf16[16,8,1792]{2,1,0:T(8,128)(2,1)} %bitcast.7, bf16[16,8,1792]{2,1,0:T(8,128)(2,1)} %bitcast.6, bf16[16,8,1792]{2,1,0:T(8,128)(2,1)} %bitcast.5, bf16[16,8,1792]{2,1,0:T(8,128)(2,1)} %bitcast.4), kind=kLoop, calls=%fused_computation.5 | loop fusion | flops 7340032 | bytes 3670016 | tf_op jit(solution)/shard_map/concatenate | solution.py:307
  34.0 8.7 %all-to-all-done = bf16[16,8,5376]{2,1,0:T(8,128)(2,1)S(1)} async-done(((bf16[16,8,5376]{2,1,0:T(8,128)(2,1)}), bf16[16,8,5376]{2,1,0:T(8,128)(2,1)S(1)}, u32[]{:S(2)}, u32[]{:S(2)}) %all-to-all-start) | async-done | bytes 1376288 | tf_op jit(solution)/shard_map/all_to_all | solution.py:30
  42.6 4.4 %all-to-all-start.1 = ((bf16[16,8,7168]{2,1,0:T(8,128)(2,1)}), bf16[16,8,7168]{2,1,0:T(8,128)(2,1)}, u32[]{:S(2)}, u32[]{:S(2)}) async-start(bf16[16,8,7168]{2,1,0:T(8,128)(2,1)} %fusion), calls=%async_computation.1 | async-start | bytes 3670016 | tf_op jit(solution)/shard_map/all_to_all | solution.py:30
  47.1 0.8 collective-permute-start.5
  47.9 2.7 %collective-permute-start.3 = (bf16[128,5376]{1,0:T(8,128)(2,1)S(1)}, bf16[128,5376]{1,0:T(8,128)(2,1)}, u32[]{:S(2)}, u32[]{:S(2)}) collective-permute-start(bf16[128,5376]{1,0:T(8,128)(2,1)S(1)} %bitcast.56), channel_id=1, source_target_pairs={{0,32},{16,112},{32,64},{48,16},{64,96},{80,48},{96,0},{112,80},{1... | collective-permute-start | bytes 4128776 | tf_op jit(solution)/shard_map/ppermute | solution.py:35
  50.6 30.2 %collective-permute-done.4.refs_4_ = bf16[128,5376]{1,0:T(8,128)(2,1)S(1)} collective-permute-done((bf16[128,5376]{1,0:T(8,128)(2,1)S(1)}, bf16[128,5376]{1,0:T(8,128)(2,1)S(1)}, u32[]{:S(2)}, u32[]{:S(2)}) %collective-permute-start.4) | collective-permute-done | bytes 1376288 | tf_op jit(solution)/shard_map/ppermute | solution.py:35
  80.8 1.1 copy-done.5
  81.9 0.1 collective-permute-start.10
  82.0 0.5 collective-permute-start.9
  82.5 2.7 %collective-permute-start.7 = (bf16[128,7168]{1,0:T(8,128)(2,1)}, bf16[128,7168]{1,0:T(8,128)(2,1)}, u32[]{:S(2)}, u32[]{:S(2)}) collective-permute-start(bf16[128,7168]{1,0:T(8,128)(2,1)} %bitcast.18.refs_6_), channel_id=1, source_target_pairs={{0,32},{16,112},{32,64},{48,16},{64,96},{80,48},{96,0},{112,80},{1... | collective-permute-start | bytes 5505032 | tf_op jit(solution)/shard_map/ppermute | solution.py:35
  85.2 6.7 %all-to-all-start.2 = ((bf16[16,8,7168]{2,1,0:T(8,128)(2,1)}), bf16[16,8,7168]{2,1,0:T(8,128)(2,1)S(1)}, u32[]{:S(2)}, u32[]{:S(2)}) async-start(bf16[16,8,7168]{2,1,0:T(8,128)(2,1)} %pad_maximum_fusion), calls=%async_computation.2 | async-start | bytes 3670016 | tf_op jit(solution)/shard_map/all_to_all | solution.py:30
  92.0 0.1 collective-permute-start.11
  92.1 0.6 collective-permute-start.6
  92.7 2.6 %collective-permute-done.11.refs_7_ = bf16[128,5376]{1,0:T(8,128)(2,1)} collective-permute-done((bf16[128,5376]{1,0:T(8,128)(2,1)S(1)}, bf16[128,5376]{1,0:T(8,128)(2,1)}, u32[]{:S(2)}, u32[]{:S(2)}) %collective-permute-start.11) | collective-permute-done | bytes 1376288 | tf_op jit(solution)/shard_map/ppermute | solution.py:26
  95.3 9.0 %shard_map.102.refs_4_ = f32[1024,512]{1,0:T(8,128)} custom-call(bf16[1,7168,256]{2,1,0:T(8,128)(2,1)} %refs_0_.5, bf16[1,7168,256]{2,1,0:T(8,128)(2,1)} %refs_1_.6, bf16[128,5376]{1,0:T(8,128)(2,1)} %bitcast.57, bf16[128,5376]{1,0:T(8,128)(2,1)} %collective-permute-done.3.refs_3_, bf16[128,5376]{1,0:T(8,128)(2,1)} %copy-done.5, ...), custom_call_target="tpu_custom_call" | custom-call | flops 1 | bytes 1 | tf_op jit(solution)/shard_map/pallas_call | solution.py:75
  104.3 35.3 %collective-permute-done.6.refs_2_.refs_8_ = bf16[128,5376]{1,0:T(8,128)(2,1)} collective-permute-done((bf16[128,5376]{1,0:T(8,128)(2,1)}, bf16[128,5376]{1,0:T(8,128)(2,1)}, u32[]{:S(2)}, u32[]{:S(2)}) %collective-permute-start.6) | collective-permute-done | bytes 1376288 | tf_op jit(solution)/shard_map/ppermute | solution.py:35
  139.7 1.7 collective-permute-start.14
  141.3 0.1 collective-permute-start.12
  141.4 0.4 collective-permute-start.15
  141.9 0.1 collective-permute-start.13
  141.9 10.4 %collective-permute-done.13.refs_3_.refs_9_ = bf16[128,5376]{1,0:T(8,128)(2,1)} collective-permute-done((bf16[128,5376]{1,0:T(8,128)(2,1)}, bf16[128,5376]{1,0:T(8,128)(2,1)}, u32[]{:S(2)}, u32[]{:S(2)}) %collective-permute-start.13) | collective-permute-done | bytes 1376288 | tf_op jit(solution)/shard_map/ppermute | solution.py:26
  152.3 5.6 %shard_map.103.refs_10_ = f32[1024,512]{1,0:T(8,128)} custom-call(bf16[1,7168,256]{2,1,0:T(8,128)(2,1)} %refs_0_.5, bf16[1,7168,256]{2,1,0:T(8,128)(2,1)} %refs_1_.6, bf16[128,5376]{1,0:T(8,128)(2,1)} %collective-permute-done.6.refs_2_.refs_8_, bf16[128,5376]{1,0:T(8,128)(2,1)} %collective-permute-done.13.refs_3_.refs_9_, ...), custom_call_target="tpu_custom_call", output_to_operand_aliasing={{}: (4, {})} | custom-call | flops 1 | bytes 1 | tf_op jit(solution)/shard_map/pallas_call | solution.py:75
  157.9 7.9 %shard_map.104 = (f32[1024,256]{1,0:T(8,128)}, f32[1024,256]{1,0:T(8,128)}, bf16[1024,256]{1,0:T(8,128)(2,1)}, bf16[256,1024]{1,0:T(8,128)(2,1)}) custom-call(bf16[1,7168,256]{2,1,0:T(8,128)(2,1)} %refs_0_.5, bf16[1,7168,256]{2,1,0:T(8,128)(2,1)} %refs_1_.6, bf16[128,7168]{1,0:T(8,128)(2,1)} %bitcast.46, bf16[128,7168]{1,0:T(8,128)(2,1)} %bitcast.47, ...), custom_call_target="tpu_custom_call" | custom-call | flops 1 | bytes 1 | tf_op jit(solution)/shard_map/pallas_call | solution.py:127
  165.8 0.8 collective-permute-start.17
  166.7 3.6 %collective-permute-done.17.refs_13_ = bf16[128,7168]{1,0:T(8,128)(2,1)S(1)} collective-permute-done((bf16[128,7168]{1,0:T(8,128)(2,1)}, bf16[128,7168]{1,0:T(8,128)(2,1)S(1)}, u32[]{:S(2)}, u32[]{:S(2)}) %collective-permute-start.17) | collective-permute-done | bytes 1835040 | tf_op jit(solution)/shard_map/ppermute | solution.py:26
  170.3 1.2 copy-done.7
  171.5 14.7 %shard_map.105 = (bf16[1,256,7168]{2,1,0:T(8,128)(2,1)}, bf16[1024,256]{1,0:T(8,128)(2,1)}, bf16[1024,256]{1,0:T(8,128)(2,1)}, f32[8,128]{1,0:T(8,128)}) custom-call(s32[8]{0:T(128)} %stack.35.refs_0_, bf16[1,256,7168]{2,1,0:T(8,128)(2,1)} %refs_1_.7, bf16[256,1024]{1,0:T(8,128)(2,1)} %get-tuple-element.43.refs_2_, f32[1024,256]{1,0:T(8,128)} %get-tuple-element.44.refs_3_, ...), custom_call_target="tpu_custom_call" | custom-call | flops 1 | bytes 1 | tf_op jit(solution)/shard_map/pallas_call | solution.py:196
  186.2 1.4 all_to_all.18
  187.6 6.9 %all-to-all-start.3 = ((f32[128,1,8]{2,1,0:T(1,128)}), f32[128,1,8]{2,1,0:T(1,128)S(1)}, u32[]{:S(2)}, u32[]{:S(2)}) async-start(f32[128,1,8]{2,1,0:T(1,128)} %bitcast.20), calls=%async_computation.3 | async-start | bytes 131072 | tf_op jit(solution)/shard_map/all_to_all | solution.py:259
  194.5 13.9 %shard_map.106 = (bf16[1,7168,256]{2,1,0:T(8,128)(2,1)}, bf16[1,7168,256]{2,1,0:T(8,128)(2,1)}) custom-call(bf16[1024,256]{1,0:T(8,128)(2,1)} %get-tuple-element.52.refs_0_, bf16[1024,256]{1,0:T(8,128)(2,1)} %get-tuple-element.53.refs_1_, bf16[128,5376]{1,0:T(8,128)(2,1)} %bitcast.58, bf16[128,5376]{1,0:T(8,128)(2,1)} %collective-permute-done.3.refs_3_, ...), custom_call_target="tpu_custom_call" | custom-call | flops 1 | bytes 1 | tf_op jit(solution)/shard_map/pallas_call | solution.py:239
  208.5 0.1 select_reduce_fusion
  208.6 0.1 fusion.5
  208.7 0.6 convert_divide_fusion
  (43 shorter events, 0.3 us)
Async XLA Ops:
  0.6 21.3 %copy-start = (bf16[128,7168]{1,0:T(8,128)(2,1)S(1)}, bf16[128,7168]{1,0:T(8,128)(2,1)}, u32[]{:S(2)}) copy-start(bf16[128,7168]{1,0:T(8,128)(2,1)} %param.8) | copy-start | bytes 5505028
  4.2 14.3 %collective-permute-start = (bf16[128,1792]{1,0:T(8,128)(2,1)}, bf16[128,1792]{1,0:T(8,128)(2,1)}, u32[]{:S(2)}, u32[]{:S(2)}) collective-permute-start(bf16[128,1792]{1,0:T(8,128)(2,1)} %convolution_convert_fusion.2), channel_id=1, source_target_pairs={{0,32},{16,112},{32,64},{48,16},{64,96},{80,48},{96,0},{112,80},{1... | collective-permute-start | bytes 1376264 | tf_op jit(solution)/shard_map/ppermute | solution.py:35
  10.5 10.7 %copy-start.9 = (bf16[128,8]{0,1:T(8,128)(2,1)S(1)}, bf16[128,8]{0,1:T(8,128)(2,1)}, u32[]{:S(2)}) copy-start(bf16[128,8]{0,1:T(8,128)(2,1)} %param.10) | copy-start | bytes 6148
  10.5 11.3 %copy-start.8 = (s32[128,8]{0,1:T(8,128)S(1)}, s32[128,8]{0,1:T(8,128)}, u32[]{:S(2)}) copy-start(s32[128,8]{0,1:T(8,128)} %param.9) | copy-start | bytes 12292
  10.5 32.1 %all-to-all-start = ((bf16[16,8,5376]{2,1,0:T(8,128)(2,1)}), bf16[16,8,5376]{2,1,0:T(8,128)(2,1)S(1)}, u32[]{:S(2)}, u32[]{:S(2)}) async-start(bf16[16,8,5376]{2,1,0:T(8,128)(2,1)} %fusion.1), calls=%async_computation | async-start | bytes 2752512 | tf_op jit(solution)/shard_map/all_to_all | solution.py:30
  18.4 11.9 %collective-permute-start.1 = (bf16[128,1792]{1,0:T(8,128)(2,1)}, bf16[128,1792]{1,0:T(8,128)(2,1)}, u32[]{:S(2)}, u32[]{:S(2)}) collective-permute-start(bf16[128,1792]{1,0:T(8,128)(2,1)} %convolution_convert_fusion.2), channel_id=1, source_target_pairs={{0,96},{16,48},{32,0},{48,80},{64,32},{80,112},{96,64},{112,16},{1... | collective-permute-start | bytes 1376264 | tf_op jit(solution)/shard_map/ppermute | solution.py:35
  18.5 12.6 %collective-permute-start.2 = (bf16[128,1792]{1,0:T(8,128)(2,1)}, bf16[128,1792]{1,0:T(8,128)(2,1)}, u32[]{:S(2)}, u32[]{:S(2)}) collective-permute-start(bf16[128,1792]{1,0:T(8,128)(2,1)} %collective-permute-done), channel_id=1, source_target_pairs={{0,32},{16,112},{32,64},{48,16},{64,96},{80,48},{96,0},{112,80},{1... | collective-permute-start | bytes 1376264 | tf_op jit(solution)/shard_map/ppermute | solution.py:35
  42.6 5.3 %copy-start.3 = (bf16[16,8,5376]{2,1,0:T(8,128)(2,1)}, bf16[16,8,5376]{2,1,0:T(8,128)(2,1)S(1)}, u32[]{:S(2)}) copy-start(bf16[16,8,5376]{2,1,0:T(8,128)(2,1)S(1)} %all-to-all-done) | copy-start | bytes 4128772
  42.6 39.3 %all-to-all-start.1 = ((bf16[16,8,7168]{2,1,0:T(8,128)(2,1)}), bf16[16,8,7168]{2,1,0:T(8,128)(2,1)}, u32[]{:S(2)}, u32[]{:S(2)}) async-start(bf16[16,8,7168]{2,1,0:T(8,128)(2,1)} %fusion), calls=%async_computation.1 | async-start | bytes 3670016 | tf_op jit(solution)/shard_map/all_to_all | solution.py:30
  47.1 3.6 %collective-permute-start.5 = (bf16[128,5376]{1,0:T(8,128)(2,1)S(1)}, bf16[128,5376]{1,0:T(8,128)(2,1)S(1)}, u32[]{:S(2)}, u32[]{:S(2)}) collective-permute-start(bf16[128,5376]{1,0:T(8,128)(2,1)S(1)} %bitcast.54), channel_id=1, source_target_pairs={{0,16},{16,0},{1,17},{17,1},{2,18},{18,2},{3,19},{19,3},{4,20},{20... | collective-permute-start | bytes 4128776 | tf_op jit(solution)/shard_map/ppermute | solution.py:26
  47.9 32.9 %collective-permute-start.4 = (bf16[128,5376]{1,0:T(8,128)(2,1)S(1)}, bf16[128,5376]{1,0:T(8,128)(2,1)S(1)}, u32[]{:S(2)}, u32[]{:S(2)}) collective-permute-start(bf16[128,5376]{1,0:T(8,128)(2,1)S(1)} %bitcast.55), channel_id=1, source_target_pairs={{0,96},{16,48},{32,0},{48,80},{64,32},{80,112},{96,64},{112,16},{1... | collective-permute-start | bytes 4128776 | tf_op jit(solution)/shard_map/ppermute | solution.py:35
  47.9 34.0 %collective-permute-start.3 = (bf16[128,5376]{1,0:T(8,128)(2,1)S(1)}, bf16[128,5376]{1,0:T(8,128)(2,1)}, u32[]{:S(2)}, u32[]{:S(2)}) collective-permute-start(bf16[128,5376]{1,0:T(8,128)(2,1)S(1)} %bitcast.56), channel_id=1, source_target_pairs={{0,32},{16,112},{32,64},{48,16},{64,96},{80,48},{96,0},{112,80},{1... | collective-permute-start | bytes 4128776 | tf_op jit(solution)/shard_map/ppermute | solution.py:35
  50.6 30.2 %copy-start.4 = (bf16[128,5376]{1,0:T(8,128)(2,1)}, bf16[128,5376]{1,0:T(8,128)(2,1)S(1)}, u32[]{:S(2)}) copy-start(bf16[128,5376]{1,0:T(8,128)(2,1)S(1)} %collective-permute-done.5.refs_5_) | copy-start | bytes 4128772
  80.8 1.1 copy-start.5
  81.9 10.0 %copy-start.6 = (bf16[128,5376]{1,0:T(8,128)(2,1)S(1)}, bf16[128,5376]{1,0:T(8,128)(2,1)}, u32[]{:S(2)}) copy-start(bf16[128,5376]{1,0:T(8,128)(2,1)} %copy-done.5) | copy-start | bytes 4128772
  81.9 10.1 %collective-permute-start.10 = (bf16[128,5376]{1,0:T(8,128)(2,1)}, bf16[128,5376]{1,0:T(8,128)(2,1)}, u32[]{:S(2)}, u32[]{:S(2)}) collective-permute-start(bf16[128,5376]{1,0:T(8,128)(2,1)} %collective-permute-done.3.refs_3_), channel_id=1, source_target_pairs={{0,16},{16,0},{1,17},{17,1},{2,18},{18,2},{3,19},{19,3},{4,20},{20... | collective-permute-start | bytes 4128776 | tf_op jit(solution)/shard_map/ppermute | solution.py:26
  82.0 57.6 %collective-permute-start.9 = (bf16[128,7168]{1,0:T(8,128)(2,1)}, bf16[128,7168]{1,0:T(8,128)(2,1)}, u32[]{:S(2)}, u32[]{:S(2)}) collective-permute-start(bf16[128,7168]{1,0:T(8,128)(2,1)} %bitcast.18.refs_6_), channel_id=1, source_target_pairs={{0,16},{16,0},{1,17},{17,1},{2,18},{18,2},{3,19},{19,3},{4,20},{20... | collective-permute-start | bytes 5505032 | tf_op jit(solution)/shard_map/ppermute | solution.py:26
  82.5 57.1 %collective-permute-start.8 = (bf16[128,7168]{1,0:T(8,128)(2,1)}, bf16[128,7168]{1,0:T(8,128)(2,1)}, u32[]{:S(2)}, u32[]{:S(2)}) collective-permute-start(bf16[128,7168]{1,0:T(8,128)(2,1)} %bitcast.18.refs_6_), channel_id=1, source_target_pairs={{0,96},{16,48},{32,0},{48,80},{64,32},{80,112},{96,64},{112,16},{1... | collective-permute-start | bytes 5505032 | tf_op jit(solution)/shard_map/ppermute | solution.py:35
  82.5 57.1 %collective-permute-start.7 = (bf16[128,7168]{1,0:T(8,128)(2,1)}, bf16[128,7168]{1,0:T(8,128)(2,1)}, u32[]{:S(2)}, u32[]{:S(2)}) collective-permute-start(bf16[128,7168]{1,0:T(8,128)(2,1)} %bitcast.18.refs_6_), channel_id=1, source_target_pairs={{0,32},{16,112},{32,64},{48,16},{64,96},{80,48},{96,0},{112,80},{1... | collective-permute-start | bytes 5505032 | tf_op jit(solution)/shard_map/ppermute | solution.py:35
  85.2 54.4 %all-to-all-start.2 = ((bf16[16,8,7168]{2,1,0:T(8,128)(2,1)}), bf16[16,8,7168]{2,1,0:T(8,128)(2,1)S(1)}, u32[]{:S(2)}, u32[]{:S(2)}) async-start(bf16[16,8,7168]{2,1,0:T(8,128)(2,1)} %pad_maximum_fusion), calls=%async_computation.2 | async-start | bytes 3670016 | tf_op jit(solution)/shard_map/all_to_all | solution.py:30
  92.0 3.3 %collective-permute-start.11 = (bf16[128,5376]{1,0:T(8,128)(2,1)S(1)}, bf16[128,5376]{1,0:T(8,128)(2,1)}, u32[]{:S(2)}, u32[]{:S(2)}) collective-permute-start(bf16[128,5376]{1,0:T(8,128)(2,1)S(1)} %copy-done.6), channel_id=1, source_target_pairs={{0,16},{16,0},{1,17},{17,1},{2,18},{18,2},{3,19},{19,3},{4,20},{20... | collective-permute-start | bytes 4128776 | tf_op jit(solution)/shard_map/ppermute | solution.py:26
  92.1 47.5 %collective-permute-start.6 = (bf16[128,5376]{1,0:T(8,128)(2,1)}, bf16[128,5376]{1,0:T(8,128)(2,1)}, u32[]{:S(2)}, u32[]{:S(2)}) collective-permute-start(bf16[128,5376]{1,0:T(8,128)(2,1)} %collective-permute-done.3.refs_3_), channel_id=1, source_target_pairs={{0,32},{16,112},{32,64},{48,16},{64,96},{80,48},{96,0},{112,80},{1... | collective-permute-start | bytes 4128776 | tf_op jit(solution)/shard_map/ppermute | solution.py:35
  139.6 18.3 %copy-start.2 = (bf16[16,8,7168]{2,1,0:T(8,128)(2,1)}, bf16[16,8,7168]{2,1,0:T(8,128)(2,1)S(1)}, u32[]{:S(2)}) copy-start(bf16[16,8,7168]{2,1,0:T(8,128)(2,1)S(1)} %all-to-all-done.2) | copy-start | bytes 5505028
  139.7 26.2 %collective-permute-start.14 = (bf16[128,7168]{1,0:T(8,128)(2,1)}, bf16[128,7168]{1,0:T(8,128)(2,1)}, u32[]{:S(2)}, u32[]{:S(2)}) collective-permute-start(bf16[128,7168]{1,0:T(8,128)(2,1)} %collective-permute-done.7.refs_7_), channel_id=1, source_target_pairs={{0,16},{16,0},{1,17},{17,1},{2,18},{18,2},{3,19},{19,3},{4,20},{20... | collective-permute-start | bytes 5505032 | tf_op jit(solution)/shard_map/ppermute | solution.py:26
  141.3 16.6 %collective-permute-start.12 = (bf16[128,7168]{1,0:T(8,128)(2,1)S(1)}, bf16[128,7168]{1,0:T(8,128)(2,1)}, u32[]{:S(2)}, u32[]{:S(2)}) collective-permute-start(bf16[128,7168]{1,0:T(8,128)(2,1)S(1)} %bitcast.45), channel_id=1, source_target_pairs={{0,16},{16,0},{1,17},{17,1},{2,18},{18,2},{3,19},{19,3},{4,20},{20... | collective-permute-start | bytes 5505032 | tf_op jit(solution)/shard_map/ppermute | solution.py:26
  141.4 24.4 %collective-permute-start.15 = (bf16[128,7168]{1,0:T(8,128)(2,1)}, bf16[128,7168]{1,0:T(8,128)(2,1)}, u32[]{:S(2)}, u32[]{:S(2)}) collective-permute-start(bf16[128,7168]{1,0:T(8,128)(2,1)} %collective-permute-done.8.refs_8_), channel_id=1, source_target_pairs={{0,16},{16,0},{1,17},{17,1},{2,18},{18,2},{3,19},{19,3},{4,20},{20... | collective-permute-start | bytes 5505032 | tf_op jit(solution)/shard_map/ppermute | solution.py:26
  141.9 24.0 %collective-permute-start.16 = (bf16[128,7168]{1,0:T(8,128)(2,1)}, bf16[128,7168]{1,0:T(8,128)(2,1)}, u32[]{:S(2)}, u32[]{:S(2)}) collective-permute-start(bf16[128,7168]{1,0:T(8,128)(2,1)} %collective-permute-done.7.refs_7_), channel_id=1, source_target_pairs={{0,32},{16,112},{32,64},{48,16},{64,96},{80,48},{96,0},{112,80},{1... | collective-permute-start | bytes 5505032 | tf_op jit(solution)/shard_map/ppermute | solution.py:35
  141.9 10.5 %collective-permute-start.13 = (bf16[128,5376]{1,0:T(8,128)(2,1)}, bf16[128,5376]{1,0:T(8,128)(2,1)}, u32[]{:S(2)}, u32[]{:S(2)}) collective-permute-start(bf16[128,5376]{1,0:T(8,128)(2,1)} %collective-permute-done.6.refs_2_.refs_8_), channel_id=1, source_target_pairs={{0,16},{16,0},{1,17},{17,1},{2,18},{18,2},{3,19},{19,3},{4,20},{20... | collective-permute-start | bytes 4128776 | tf_op jit(solution)/shard_map/ppermute | solution.py:26
  165.8 4.5 %collective-permute-start.17 = (bf16[128,7168]{1,0:T(8,128)(2,1)}, bf16[128,7168]{1,0:T(8,128)(2,1)S(1)}, u32[]{:S(2)}, u32[]{:S(2)}) collective-permute-start(bf16[128,7168]{1,0:T(8,128)(2,1)} %collective-permute-done.16.refs_12_), channel_id=1, source_target_pairs={{0,16},{16,0},{1,17},{17,1},{2,18},{18,2},{3,19},{19,3},{4,20},{20... | collective-permute-start | bytes 5505032 | tf_op jit(solution)/shard_map/ppermute | solution.py:26
  170.3 1.2 copy-start.7
  187.6 20.8 %all-to-all-start.3 = ((f32[128,1,8]{2,1,0:T(1,128)}), f32[128,1,8]{2,1,0:T(1,128)S(1)}, u32[]{:S(2)}, u32[]{:S(2)}) async-start(f32[128,1,8]{2,1,0:T(1,128)} %bitcast.20), calls=%async_computation.3 | async-start | bytes 131072 | tf_op jit(solution)/shard_map/all_to_all | solution.py:259
  194.5 14.8 %copy-start.1 = (bf16[128,7168]{1,0:T(8,128)(2,1)S(1)}, bf16[128,7168]{1,0:T(8,128)(2,1)}, u32[]{:S(2)}) copy-start(bf16[128,7168]{1,0:T(8,128)(2,1)} %param.8) | copy-start | bytes 5505028
where the time goes:
time: 210 us; the launch traced here: 209 us
  waiting for transfers between devices  98.2 us (47%)
  Pallas kernels  51.1 us (24%)
  starting transfers between devices  42.6 us (20%)
  matrix products  7.03 us (3%)
  other arithmetic  4.81 us (2%)
  local copies, waits for them, and re-layouts  4.72 us (2%)
    ppermute x9, waiting for transfers between devices, hop(): return lax.ppermute(x, ('x', 'core'), pairs)  72.8 us
    all_to_all x3, starting transfers between devices, exchange_yz(): lax.all_to_all(tiles, ('z', 'y'), 0, 0, tiled=True)  19.1 us
    ppermute x9, waiting for transfers between devices, shift(): return lax.ppermute(x, axis, [(i, (i + by) % n) for i in range(n)])  16.7 us
    pallas_call x1, Pallas kernels, down_terms(): pl.pallas_call(kernel, grid=(steps,), in_specs=[pl.BlockSpec(memory_space...  14.7 us
    pallas_call x2, Pallas kernels, forward(): pl.pallas_call(kernel, grid=(size // block,), in_specs=[pl.BlockSpec((1,...  14.6 us
    pallas_call x1, Pallas kernels, up_terms(): pl.pallas_call(kernel, grid=(steps + last_steps,), in_specs=[whole, whole...  13.9 us
    ppermute x9, starting transfers between devices, hop(): return lax.ppermute(x, ('x', 'core'), pairs)  12 us
    all_to_all x3, waiting for transfers between devices, exchange_yz(): lax.all_to_all(tiles, ('z', 'y'), 0, 0, tiled=True)  8.66 us
  transfers between devices with their start and end apart: 22, of which 9 were waited for; matrix products, arithmetic and copies ran while one was open for 4% of the time, Pallas kernels for 17%

commit v1 on v0

--- a/solution.py
+++ b/solution.py
@@ -14,7 +14,7 @@
 
 X_RAW, X_REST = 1792, 5376
 BLOCK, END_BLOCK = 1792, 896
-PARAMS = pltpu.CompilerParams(vmem_limit_bytes=62 * 2**20)
+PARAMS = pltpu.CompilerParams(vmem_limit_bytes=63 * 2**20)
 
 
 def after(x, *others):
@@ -143,30 +143,60 @@
     )(w_gate, w_up, *[part[0] for part in parts], pre)
 
 
-def down_terms(parts, w_down, turned, activated, slope, hidden, order):
+def project(parts, w_down):
+    parts = whole_parts(parts)
+    size = parts[0][2]
+    rows, width = sum(part.shape[0] for part, _, _ in parts), w_down.shape[1]
+    block = math.gcd(BLOCK, size)
+
+    def kernel(down_ref, *refs):
+        out_ref = refs[-1]
+
+        @pl.when(pl.program_id(0) == 0)
+        def _():
+            out_ref[...] = jnp.zeros_like(out_ref)
+
+        out_ref[...] += lax.dot_general(
+            joined(refs[:-1]), down_ref[0], (((1,), (1,)), ((), ())), preferred_element_type=jnp.float32
+        )
+
+    return pl.pallas_call(
+        kernel,
+        grid=(size // block,),
+        in_specs=[pl.BlockSpec((1, width, block), lambda i: (0, 0, i))] + row_specs(parts, block),
+        out_specs=pl.BlockSpec((rows, width), lambda i: (0, 0)),
+        out_shape=jax.ShapeDtypeStruct((rows, width), jnp.float32),
+        compiler_params=PARAMS,
+        cost_estimate=SMALL,
+    )(w_down, *[part[0] for part in parts])
+
+
+def down_terms(parts, w_down, turned, projected, activated, slope, hidden, order):
     parts = whole_parts(parts)
     size, count = parts[0][2], len(parts)
     rows, width = hidden.shape
     block = math.gcd(BLOCK, size)
     steps = size // block
-    strip = rows // (NX * NC)
+    strip, known = rows // (NX * NC), projected.shape[0]
+    late = (activated, slope, hidden, projected)
+    n_late = len(late)
 
     def kernel(*refs):
         order_ref, down_ref, turned_ref = refs[:3]
-        late_refs = refs[3:6]
-        grad_ref, gate_ref, up_ref, row_ref, projected_ref = refs[-9:-4]
-        held, sems = refs[-4:-1], refs[-1]
+        late_refs = refs[3 : 3 + n_late]
+        grad_ref, gate_ref, up_ref, row_ref, projected_ref = refs[-6 - n_late : -1 - n_late]
+        held, sems = refs[-1 - n_late : -1], refs[-1]
         copies = [pltpu.make_async_copy(late, own, sems.at[k]) for k, (late, own) in enumerate(zip(late_refs, held))]
 
         @pl.when(pl.program_id(0) == 0)
         def _():
             for copy in copies:
                 copy.start()
-            projected_ref[...] = jnp.zeros_like(projected_ref)
-
-        dy = joined(refs[6 : 6 + count])
-        projected_ref[...] += lax.dot_general(
-            dy, down_ref[0], (((1,), (1,)), ((), ())), preferred_element_type=jnp.float32
+            projected_ref[known:] = jnp.zeros_like(projected_ref[known:])
+
+        dy = joined(refs[3 + n_late : 3 + n_late + count])
+        projected_ref[known:] += lax.dot_general(
+            dy[known:], down_ref[0], (((1,), (1,)), ((), ())), preferred_element_type=jnp.float32
         )
         grad_ref[0] = jnp.dot(turned_ref[...], dy, preferred_element_type=jnp.float32).astype(jnp.bfloat16)
 
@@ -174,37 +204,43 @@
         def _():
             for copy in copies:
                 copy.wait()
-            activated_ref, slope_ref, hidden_ref = held
-
-            def some(k, _):
-                at_rows = pl.ds(pl.multiple_of(k * strip, strip), strip)
+            activated_ref, slope_ref, hidden_ref, known_ref = held
+            projected_ref[:known] = known_ref[...]
+            row = lax.broadcasted_iota(jnp.int32, (strip // CAP, strip), 1)
+            source = lax.broadcasted_iota(jnp.int32, (strip // CAP, strip), 0)
+            of_source = (row // CAP == source).astype(jnp.float32)
+            row = lax.broadcasted_iota(jnp.int32, (strip, CAP), 0)
+            slot = lax.broadcasted_iota(jnp.int32, (strip, CAP), 1)
+            in_slot = row % CAP == slot
+
+            for k in range(rows // strip):
+                at_rows = slice(k * strip, (k + 1) * strip)
                 projected = projected_ref[at_rows]
                 gate_ref[at_rows] = (projected * slope_ref[at_rows]).astype(jnp.bfloat16)
                 up_ref[at_rows] = (projected * activated_ref[at_rows]).astype(jnp.bfloat16)
                 sums = jnp.sum(hidden_ref[at_rows].astype(jnp.float32) * projected, axis=1, keepdims=True)
-                row_ref[pl.ds(order_ref[k], 1)] = jnp.broadcast_to(sums, (strip, strip)).T[:1]
-                return 0
-
-            lax.fori_loop(0, rows // strip, some, 0)
+                place = pl.ds(pl.multiple_of(order_ref[k] * (strip // CAP), strip // CAP), strip // CAP)
+                row_ref[place] = jnp.dot(
+                    of_source, jnp.where(in_slot, sums, 0.0), precision=lax.Precision.HIGHEST
+                )
 
     def whole(*shape):
         return pl.BlockSpec(shape, lambda i: (0, 0))
 
     wide = pl.BlockSpec((1, width, block), lambda i: (0, 0, i))
     grad = jax.ShapeDtypeStruct((rows, width), jnp.bfloat16)
-    late = (activated, slope, hidden)
     return pl.pallas_call(
         kernel,
         grid=(steps,),
         in_specs=[pl.BlockSpec(memory_space=pltpu.SMEM), wide, whole(width, rows)]
         + [ANY] * len(late)
         + row_specs(parts, block),
-        out_specs=[wide, whole(rows, width), whole(rows, width), whole(NX * NC, strip)],
+        out_specs=[wide, whole(rows, width), whole(rows, width), whole(rows // CAP, CAP)],
         out_shape=[
             jax.ShapeDtypeStruct(w_down.shape, jnp.bfloat16),
             grad,
             grad,
-            jax.ShapeDtypeStruct((NX * NC, strip), jnp.float32),
+            jax.ShapeDtypeStruct((rows // CAP, CAP), jnp.float32),
         ],
         scratch_shapes=[pltpu.VMEM((rows, width), jnp.float32)]
         + [pltpu.VMEM(a.shape, a.dtype) for a in late]
@@ -256,7 +292,7 @@
 
 
 def return_rows(row_gate):
-    got = lax.all_to_all(row_gate.reshape(-1, CAP), ("x", "core", "z", "y"), 0, 0, tiled=True)
+    got = lax.all_to_all(row_gate, ("x", "core", "z", "y"), 0, 0, tiled=True)
     return jnp.sum(got.reshape(NC * NX, NZ * NY, CAP), axis=0)
 
 
@@ -302,7 +338,9 @@
     raw = tiles_of(placer, tokens, X_REST, X_RAW).reshape(-1, X_RAW)
     on_r, back_r = hop(raw, 1), hop(raw, -1)
     x = exchange_yz(after(tiles_of(placer, tokens, 0, X_REST), raw))
-    rounds = [part.reshape(columns, CAP, X_RAW) for part in (raw, on_r, back_r, hop(on_r, 1))]
+    middle = raw.shape[0] // 2
+    again_r = jnp.concatenate([hop(on_r[:middle], 1), hop(back_r[middle:], -1)])
+    rounds = [part.reshape(columns, CAP, X_RAW) for part in (raw, on_r, back_r, again_r)]
     dy = tiles_of(placer_gate, cotangent, 0, features)
     rounds = jnp.concatenate(rounds, axis=2)
 
@@ -331,10 +369,12 @@
     pre = forward(again_x, w_gate, w_up, 0, all_rows, split, pre)
     activated, slope, hidden, turned = forward_end(raw_rows, w_gate, w_up, X_REST, pre)
 
-    ties = (again_dy, *near_dy, turned)
+    known = project(near_dy[:4], w_down)
+
+    ties = (again_dy, *near_dy, turned, known)
     again_dy = (again_dy, swap(after(again_dy, *ties)))
     grad_down, grad_pre_gate, grad_pre_up, row_gate = down_terms(
-        (*near_dy, *again_dy), w_down, turned, activated, slope, hidden, order
+        (*near_dy, *again_dy), w_down, turned, known, activated, slope, hidden, order
     )
     returned = return_rows(row_gate).reshape(columns, CAP)
     grads = up_terms((*near_x, *again_x), raw_rows, grad_pre_gate, grad_pre_up)

time: 210 us -> 202 us (0.962)
  waiting for transfers between devices: 98.2 us -> 82 us
  starting transfers between devices: 42.6 us -> 50.3 us
  Pallas kernels: 51.1 us -> 55.8 us
  local copies, waits for them, and re-layouts: 4.72 us -> 1.74 us
    ppermute x9, waiting for transfers between devices: 16.7 us -> 7.31 us  [shift(): return lax.ppermute(x, axis, [(i, (i + by) % n) for i in range(n)])]
    ppermute x9 -> x10, waiting for transfers between devices: 72.8 us -> 65.1 us  [hop(): return lax.ppermute(x, ('x', 'core'), pairs)]
    pallas_call x0 -> x1, Pallas kernels: none -> 6.69 us  [project(): pl.pallas_call(kernel, grid=(size // block,), in_specs=[pl.BlockSpec((1,...]
    ppermute x9 -> x10, starting transfers between devices: 12 us -> 15 us  [hop(): return lax.ppermute(x, ('x', 'core'), pairs)]
    ppermute x9, starting transfers between devices: 4.62 us -> 7.27 us  [shift(): return lax.ppermute(x, axis, [(i, (i + by) % n) for i in range(n)])]
    unnamed x20 -> x10, local copies, waits for them, and re-layouts: 2.36 us -> 0.02 us
  transfers between devices with their start and end apart: 22 -> 23, of which waited for: 9 -> 9; matrix products, arithmetic and copies ran while one was open for 4% -> 5% of each run, Pallas kernels for 17% -> 21%
where the time goes in v1:
time: 202 us
  waiting for transfers between devices  82 us (41%)
  Pallas kernels  55.8 us (28%)
  starting transfers between devices  50.3 us (25%)
  matrix products  7.75 us (4%)
  other arithmetic  3.31 us (2%)
    ppermute x10, waiting for transfers between devices, hop(): return lax.ppermute(x, ('x', 'core'), pairs)  65.1 us
    all_to_all x3, starting transfers between devices, exchange_yz(): lax.all_to_all(tiles, ('z', 'y'), 0, 0, tiled=True)  20.5 us
    ppermute x10, starting transfers between devices, hop(): return lax.ppermute(x, ('x', 'core'), pairs)  15 us
    pallas_call x2, Pallas kernels, forward(): pl.pallas_call(kernel, grid=(size // block,), in_specs=[pl.BlockSpec((1,...  14.5 us
    pallas_call x1, Pallas kernels, up_terms(): pl.pallas_call(kernel, grid=(steps + last_steps,), in_specs=[whole, whole...  13.8 us
    pallas_call x1, Pallas kernels, down_terms(): pl.pallas_call(kernel, grid=(steps,), in_specs=[pl.BlockSpec(memory_space...  12.8 us
    all_to_all x3, waiting for transfers between devices, exchange_yz(): lax.all_to_all(tiles, ('z', 'y'), 0, 0, tiled=True)  9.58 us
    pallas_call x1, Pallas kernels, forward_end(): pl.pallas_call(kernel, grid=(steps,), in_specs=[pl.BlockSpec((1, block, w...  7.94 us
  transfers between devices with their start and end apart: 23, of which 9 were waited for; matrix products, arithmetic and copies ran while one was open for 5% of the time, Pallas kernels for 21%

profile of v1, /device:TPU:1, one launch (start us, length us, event | category | flops | bytes accessed | tf_op | source)
XLA Modules:
  0.0 201.8 jit_solution(7687475632692651843)
XLA Ops:
  0.7 0.1 eq.66
  0.7 0.8 compare_reduce_fusion
  1.5 0.1 copy.24
  1.7 0.2 reduce_window_sum.11
  2.0 1.4 convolution_convert_fusion.2
  3.3 2.1 %collective-permute-start.1 = (bf16[128,1792]{1,0:T(8,128)(2,1)S(1)}, bf16[128,1792]{1,0:T(8,128)(2,1)S(1)}, u32[]{:S(2)}, u32[]{:S(2)}) collective-permute-start(bf16[128,1792]{1,0:T(8,128)(2,1)S(1)} %convolution_convert_fusion.2), channel_id=1, source_target_pairs={{0,96},{16,48},{32,0},{48,80},{64,32},{80,112},{96,64},{112,16},{1... | collective-permute-start | bytes 1376264 | tf_op jit(solution)/shard_map/ppermute | solution.py:35
  5.5 1.3 collective-permute-start
  6.8 3.0 %fusion.1 = bf16[16,8,5376]{2,1,0:T(8,128)(2,1)} fusion(bf16[128,7168]{1,0:T(8,128)(2,1)} %param.7, s32[128]{0:T(128)S(1)} %eq.66, s32[128,16]{0,1:T(8,128)S(1)} %copy.25, pred[128,16]{0,1:T(8,128)(4,1)S(1)} %copy.26), kind=kOutput, calls=%fused_computation.3 | convolution fusion | flops 176881664 | bytes 2763264 | tf_op jit(solution)/shard_map/dot_general | solution.py:320
  9.8 8.0 %all-to-all-start = ((bf16[16,8,5376]{2,1,0:T(8,128)(2,1)}), bf16[16,8,5376]{2,1,0:T(8,128)(2,1)S(1)}, u32[]{:S(2)}, u32[]{:S(2)}) async-start(bf16[16,8,5376]{2,1,0:T(8,128)(2,1)} %fusion.1), calls=%async_computation | async-start | bytes 2752512 | tf_op jit(solution)/shard_map/all_to_all | solution.py:30
  17.9 0.1 collective-permute-start.3
  18.0 0.7 slice.16
  18.7 2.7 %collective-permute-start.2 = (bf16[64,1792]{1,0:T(8,128)(2,1)}, bf16[64,1792]{1,0:T(8,128)(2,1)S(1)}, u32[]{:S(2)}, u32[]{:S(2)}) collective-permute-start(bf16[64,1792]{1,0:T(8,128)(2,1)} %slice.16), channel_id=1, source_target_pairs={{0,32},{16,112},{32,64},{48,16},{64,96},{80,48},{96,0},{112,80},{1... | collective-permute-start | bytes 688136 | tf_op jit(solution)/shard_map/ppermute | solution.py:35
  21.3 0.1 fusion.4
  21.5 0.7 stack.35.refs_0_
  22.2 3.4 %fusion = bf16[16,8,7168]{2,1,0:T(8,128)(2,1)} fusion(bf16[128,7168]{1,0:T(8,128)(2,1)} %param.8, bf16[128,16]{0,1:T(8,128)(2,1)S(1)} %fusion.4, s32[128]{0:T(128)S(1)} %eq.66, s32[128,16]{0,1:T(8,128)S(1)} %copy.25, pred[128,16]{0,1:T(8,128)(4,1)S(1)} %copy.26), kind=kOutput, calls=%fused_computation.1 | convolution fusion | flops 235847680 | bytes 3684864 | tf_op jit(solution)/shard_map/dot_general | solution.py:320
  25.6 0.6 collective-permute-done.2
  26.3 1.4 pad_maximum_fusion
  27.7 9.6 %all-to-all-done = bf16[16,8,5376]{2,1,0:T(8,128)(2,1)S(1)} async-done(((bf16[16,8,5376]{2,1,0:T(8,128)(2,1)}), bf16[16,8,5376]{2,1,0:T(8,128)(2,1)S(1)}, u32[]{:S(2)}, u32[]{:S(2)}) %all-to-all-start) | async-done | bytes 1376288 | tf_op jit(solution)/shard_map/all_to_all | solution.py:30
  37.3 5.7 %all-to-all-start.1 = ((bf16[16,8,7168]{2,1,0:T(8,128)(2,1)}), bf16[16,8,7168]{2,1,0:T(8,128)(2,1)}, u32[]{:S(2)}, u32[]{:S(2)}) async-start(bf16[16,8,7168]{2,1,0:T(8,128)(2,1)} %fusion), calls=%async_computation.1 | async-start | bytes 3670016 | tf_op jit(solution)/shard_map/all_to_all | solution.py:30
  42.9 2.0 collective-permute-start.6
  44.9 2.7 %collective-permute-start.4 = (bf16[128,5376]{1,0:T(8,128)(2,1)S(1)}, bf16[128,5376]{1,0:T(8,128)(2,1)}, u32[]{:S(2)}, u32[]{:S(2)}) collective-permute-start(bf16[128,5376]{1,0:T(8,128)(2,1)S(1)} %bitcast.50), channel_id=1, source_target_pairs={{0,32},{16,112},{32,64},{48,16},{64,96},{80,48},{96,0},{112,80},{1... | collective-permute-start | bytes 4128776 | tf_op jit(solution)/shard_map/ppermute | solution.py:35
  47.6 0.1 collective-permute-done.6.refs_5_
  47.6 28.8 %collective-permute-done.5.refs_4_ = bf16[128,5376]{1,0:T(8,128)(2,1)S(1)} collective-permute-done((bf16[128,5376]{1,0:T(8,128)(2,1)S(1)}, bf16[128,5376]{1,0:T(8,128)(2,1)S(1)}, u32[]{:S(2)}, u32[]{:S(2)}) %collective-permute-start.5) | collective-permute-done | bytes 1376288 | tf_op jit(solution)/shard_map/ppermute | solution.py:35
  76.5 0.3 collective-permute-done.4.refs_3_
  76.8 2.0 %collective-permute-start.11 = (bf16[128,5376]{1,0:T(8,128)(2,1)}, bf16[128,5376]{1,0:T(8,128)(2,1)}, u32[]{:S(2)}, u32[]{:S(2)}) collective-permute-start(bf16[128,5376]{1,0:T(8,128)(2,1)} %collective-permute-done.4.refs_3_), channel_id=1, source_target_pairs={{0,16},{16,0},{1,17},{17,1},{2,18},{18,2},{3,19},{19,3},{4,20},{20... | collective-permute-start | bytes 4128776 | tf_op jit(solution)/shard_map/ppermute | solution.py:26
  78.8 2.7 %collective-permute-start.8 = (bf16[128,7168]{1,0:T(8,128)(2,1)}, bf16[128,7168]{1,0:T(8,128)(2,1)}, u32[]{:S(2)}, u32[]{:S(2)}) collective-permute-start(bf16[128,7168]{1,0:T(8,128)(2,1)} %bitcast.18.refs_0_.refs_7_), channel_id=1, source_target_pairs={{0,32},{16,112},{32,64},{48,16},{64,96},{80,48},{96,0},{112,80},{1... | collective-permute-start | bytes 5505032 | tf_op jit(solution)/shard_map/ppermute | solution.py:35
  81.5 6.8 %all-to-all-start.2 = ((bf16[16,8,7168]{2,1,0:T(8,128)(2,1)}), bf16[16,8,7168]{2,1,0:T(8,128)(2,1)}, u32[]{:S(2)}, u32[]{:S(2)}) async-start(bf16[16,8,7168]{2,1,0:T(8,128)(2,1)} %pad_maximum_fusion), calls=%async_computation.2 | async-start | bytes 3670016 | tf_op jit(solution)/shard_map/all_to_all | solution.py:30
  88.3 0.2 collective-permute-start.12
  88.5 2.1 %collective-permute-start.7 = (bf16[128,5376]{1,0:T(8,128)(2,1)}, bf16[128,5376]{1,0:T(8,128)(2,1)}, u32[]{:S(2)}, u32[]{:S(2)}) collective-permute-start(bf16[128,5376]{1,0:T(8,128)(2,1)} %collective-permute-done.4.refs_3_), channel_id=1, source_target_pairs={{0,32},{16,112},{32,64},{48,16},{64,96},{80,48},{96,0},{112,80},{1... | collective-permute-start | bytes 4128776 | tf_op jit(solution)/shard_map/ppermute | solution.py:35
  90.6 1.0 collective-permute-done.12.refs_7_
  91.6 9.0 %shard_map.102.refs_4_ = f32[1024,512]{1,0:T(8,128)} custom-call(bf16[1,7168,256]{2,1,0:T(8,128)(2,1)} %refs_0_.5, bf16[1,7168,256]{2,1,0:T(8,128)(2,1)} %refs_1_.6, bf16[128,5376]{1,0:T(8,128)(2,1)} %bitcast.51, bf16[128,5376]{1,0:T(8,128)(2,1)} %collective-permute-done.4.refs_3_, bf16[128,5376]{1,0:T(8,128)(2,1)} %copy-done.2, ...), custom_call_target="tpu_custom_call" | custom-call | flops 1 | bytes 1 | tf_op jit(solution)/shard_map/pallas_call | solution.py:75
  100.6 35.3 %collective-permute-done.7.refs_2_.refs_8_ = bf16[128,5376]{1,0:T(8,128)(2,1)} collective-permute-done((bf16[128,5376]{1,0:T(8,128)(2,1)}, bf16[128,5376]{1,0:T(8,128)(2,1)}, u32[]{:S(2)}, u32[]{:S(2)}) %collective-permute-start.7) | collective-permute-done | bytes 1376288 | tf_op jit(solution)/shard_map/ppermute | solution.py:35
  135.9 1.7 collective-permute-start.15
  137.6 0.1 collective-permute-start.13
  137.7 0.4 collective-permute-start.16
  138.1 1.3 collective-permute-start.17
  139.4 6.7 %shard_map.105.refs_6_ = f32[512,256]{1,0:T(8,128)} custom-call(bf16[1,256,7168]{2,1,0:T(8,128)(2,1)} %refs_1_.7, bf16[128,7168]{1,0:T(8,128)(2,1)} %bitcast.18.refs_0_.refs_7_, bf16[128,7168]{1,0:T(8,128)(2,1)} %collective-permute-done.8.refs_1_.refs_8_, bf16[128,7168]{1,0:T(8,128)(2,1)} %collective-permute-done.9.refs_2_.refs_9_, ...), custom_call_target="tpu_custom_call" | custom-call | flops 1 | bytes 1 | tf_op jit(solution)/shard_map/pallas_call | solution.py:163
  146.1 2.5 %collective-permute-done.14.refs_3_.refs_9_ = bf16[128,5376]{1,0:T(8,128)(2,1)} collective-permute-done((bf16[128,5376]{1,0:T(8,128)(2,1)}, bf16[128,5376]{1,0:T(8,128)(2,1)}, u32[]{:S(2)}, u32[]{:S(2)}) %collective-permute-start.14) | collective-permute-done | bytes 1376288 | tf_op jit(solution)/shard_map/ppermute | solution.py:26
  148.6 5.6 %shard_map.103.refs_10_ = f32[1024,512]{1,0:T(8,128)} custom-call(bf16[1,7168,256]{2,1,0:T(8,128)(2,1)} %refs_0_.5, bf16[1,7168,256]{2,1,0:T(8,128)(2,1)} %refs_1_.6, bf16[128,5376]{1,0:T(8,128)(2,1)} %collective-permute-done.7.refs_2_.refs_8_, bf16[128,5376]{1,0:T(8,128)(2,1)} %collective-permute-done.14.refs_3_.refs_9_, ...), custom_call_target="tpu_custom_call", output_to_operand_aliasing={{}: (4, {})} | custom-call | flops 1 | bytes 1 | tf_op jit(solution)/shard_map/pallas_call | solution.py:75
  154.2 7.9 %shard_map.104 = (f32[1024,256]{1,0:T(8,128)}, f32[1024,256]{1,0:T(8,128)}, bf16[1024,256]{1,0:T(8,128)(2,1)}, bf16[256,1024]{1,0:T(8,128)(2,1)}) custom-call(bf16[1,7168,256]{2,1,0:T(8,128)(2,1)} %refs_0_.5, bf16[1,7168,256]{2,1,0:T(8,128)(2,1)} %refs_1_.6, bf16[128,7168]{1,0:T(8,128)(2,1)} %bitcast.19.refs_2_.refs_3_.refs_4_.refs_8_.refs_10_.refs_11_.refs_12_.refs_16_, ...), custom_call_target="tpu_custom_call" | custom-call | flops 1 | bytes 1 | tf_op jit(solution)/shard_map/pallas_call | solution.py:127
  162.1 0.8 collective-permute-start.18
  163.0 3.8 %collective-permute-done.18.refs_14_ = bf16[128,7168]{1,0:T(8,128)(2,1)} collective-permute-done((bf16[128,7168]{1,0:T(8,128)(2,1)}, bf16[128,7168]{1,0:T(8,128)(2,1)}, u32[]{:S(2)}, u32[]{:S(2)}) %collective-permute-start.18) | collective-permute-done | bytes 1835040 | tf_op jit(solution)/shard_map/ppermute | solution.py:26
  166.7 12.8 %shard_map.106 = (bf16[1,256,7168]{2,1,0:T(8,128)(2,1)}, bf16[1024,256]{1,0:T(8,128)(2,1)}, bf16[1024,256]{1,0:T(8,128)(2,1)}, f32[128,8]{1,0:T(8,128)}) custom-call(s32[8]{0:T(128)} %stack.35.refs_0_, bf16[1,256,7168]{2,1,0:T(8,128)(2,1)} %refs_1_.7, bf16[256,1024]{1,0:T(8,128)(2,1)} %get-tuple-element.43.refs_2_, f32[1024,256]{1,0:T(8,128)} %get-tuple-element.44.refs_3_, ...), custom_call_target="tpu_custom_call" | custom-call | flops 1 | bytes 1 | tf_op jit(solution)/shard_map/pallas_call | solution.py:232
  179.5 7.6 %all-to-all-start.3 = ((f32[128,1,8]{2,1,0:T(1,128)}), f32[128,1,8]{2,1,0:T(1,128)S(1)}, u32[]{:S(2)}, u32[]{:S(2)}) async-start(f32[128,1,8]{2,1,0:T(1,128)} %bitcast.57), calls=%async_computation.3 | async-start | bytes 131072 | tf_op jit(solution)/shard_map/all_to_all | solution.py:295
  187.1 13.8 %shard_map.107 = (bf16[1,7168,256]{2,1,0:T(8,128)(2,1)}, bf16[1,7168,256]{2,1,0:T(8,128)(2,1)}) custom-call(bf16[1024,256]{1,0:T(8,128)(2,1)} %get-tuple-element.52.refs_0_, bf16[1024,256]{1,0:T(8,128)(2,1)} %get-tuple-element.53.refs_1_, bf16[128,5376]{1,0:T(8,128)(2,1)} %bitcast.52, bf16[128,5376]{1,0:T(8,128)(2,1)} %collective-permute-done.4.refs_3_, ...), custom_call_target="tpu_custom_call" | custom-call | flops 1 | bytes 1 | tf_op jit(solution)/shard_map/pallas_call | solution.py:275
  201.0 0.1 select_reduce_fusion
  201.1 0.1 fusion.5
  201.2 0.6 convert_divide_fusion
  (38 shorter events, 0.3 us)
Async XLA Ops:
  3.3 14.5 %collective-permute-start.1 = (bf16[128,1792]{1,0:T(8,128)(2,1)S(1)}, bf16[128,1792]{1,0:T(8,128)(2,1)S(1)}, u32[]{:S(2)}, u32[]{:S(2)}) collective-permute-start(bf16[128,1792]{1,0:T(8,128)(2,1)S(1)} %convolution_convert_fusion.2), channel_id=1, source_target_pairs={{0,96},{16,48},{32,0},{48,80},{64,32},{80,112},{96,64},{112,16},{1... | collective-permute-start | bytes 1376264 | tf_op jit(solution)/shard_map/ppermute | solution.py:35
  5.5 12.5 %collective-permute-start = (bf16[128,1792]{1,0:T(8,128)(2,1)S(1)}, bf16[128,1792]{1,0:T(8,128)(2,1)S(1)}, u32[]{:S(2)}, u32[]{:S(2)}) collective-permute-start(bf16[128,1792]{1,0:T(8,128)(2,1)S(1)} %convolution_convert_fusion.2), channel_id=1, source_target_pairs={{0,32},{16,112},{32,64},{48,16},{64,96},{80,48},{96,0},{112,80},{1... | collective-permute-start | bytes 1376264 | tf_op jit(solution)/shard_map/ppermute | solution.py:35
  9.8 8.0 %copy-start.4 = (bf16[128,8]{0,1:T(8,128)(2,1)S(1)}, bf16[128,8]{0,1:T(8,128)(2,1)}, u32[]{:S(2)}) copy-start(bf16[128,8]{0,1:T(8,128)(2,1)} %param.10) | copy-start | bytes 6148
  9.8 11.5 %copy-start.3 = (s32[128,8]{0,1:T(8,128)S(1)}, s32[128,8]{0,1:T(8,128)}, u32[]{:S(2)}) copy-start(s32[128,8]{0,1:T(8,128)} %param.9) | copy-start | bytes 12292
  9.8 27.5 %all-to-all-start = ((bf16[16,8,5376]{2,1,0:T(8,128)(2,1)}), bf16[16,8,5376]{2,1,0:T(8,128)(2,1)S(1)}, u32[]{:S(2)}, u32[]{:S(2)}) async-start(bf16[16,8,5376]{2,1,0:T(8,128)(2,1)} %fusion.1), calls=%async_computation | async-start | bytes 2752512 | tf_op jit(solution)/shard_map/all_to_all | solution.py:30
  17.9 7.7 %collective-permute-start.3 = (bf16[64,1792]{1,0:T(8,128)(2,1)S(1)}, bf16[64,1792]{1,0:T(8,128)(2,1)S(1)}, u32[]{:S(2)}, u32[]{:S(2)}) collective-permute-start(bf16[64,1792]{1,0:T(8,128)(2,1)S(1)} %slice.17), channel_id=1, source_target_pairs={{0,96},{16,48},{32,0},{48,80},{64,32},{80,112},{96,64},{112,16},{1... | collective-permute-start | bytes 688136 | tf_op jit(solution)/shard_map/ppermute | solution.py:35
  18.7 7.6 %collective-permute-start.2 = (bf16[64,1792]{1,0:T(8,128)(2,1)}, bf16[64,1792]{1,0:T(8,128)(2,1)S(1)}, u32[]{:S(2)}, u32[]{:S(2)}) collective-permute-start(bf16[64,1792]{1,0:T(8,128)(2,1)} %slice.16), channel_id=1, source_target_pairs={{0,32},{16,112},{32,64},{48,16},{64,96},{80,48},{96,0},{112,80},{1... | collective-permute-start | bytes 688136 | tf_op jit(solution)/shard_map/ppermute | solution.py:35
  37.3 7.6 %copy-start = (bf16[16,8,5376]{2,1,0:T(8,128)(2,1)}, bf16[16,8,5376]{2,1,0:T(8,128)(2,1)S(1)}, u32[]{:S(2)}) copy-start(bf16[16,8,5376]{2,1,0:T(8,128)(2,1)S(1)} %all-to-all-done) | copy-start | bytes 4128772
  37.3 39.5 %all-to-all-start.1 = ((bf16[16,8,7168]{2,1,0:T(8,128)(2,1)}), bf16[16,8,7168]{2,1,0:T(8,128)(2,1)}, u32[]{:S(2)}, u32[]{:S(2)}) async-start(bf16[16,8,7168]{2,1,0:T(8,128)(2,1)} %fusion), calls=%async_computation.1 | async-start | bytes 3670016 | tf_op jit(solution)/shard_map/all_to_all | solution.py:30
  42.9 4.7 %collective-permute-start.6 = (bf16[128,5376]{1,0:T(8,128)(2,1)S(1)}, bf16[128,5376]{1,0:T(8,128)(2,1)S(1)}, u32[]{:S(2)}, u32[]{:S(2)}) collective-permute-start(bf16[128,5376]{1,0:T(8,128)(2,1)S(1)} %bitcast.48), channel_id=1, source_target_pairs={{0,16},{16,0},{1,17},{17,1},{2,18},{18,2},{3,19},{19,3},{4,20},{20... | collective-permute-start | bytes 4128776 | tf_op jit(solution)/shard_map/ppermute | solution.py:26
  44.9 31.6 %collective-permute-start.5 = (bf16[128,5376]{1,0:T(8,128)(2,1)S(1)}, bf16[128,5376]{1,0:T(8,128)(2,1)S(1)}, u32[]{:S(2)}, u32[]{:S(2)}) collective-permute-start(bf16[128,5376]{1,0:T(8,128)(2,1)S(1)} %bitcast.49), channel_id=1, source_target_pairs={{0,96},{16,48},{32,0},{48,80},{64,32},{80,112},{96,64},{112,16},{1... | collective-permute-start | bytes 4128776 | tf_op jit(solution)/shard_map/ppermute | solution.py:35
  44.9 31.9 %collective-permute-start.4 = (bf16[128,5376]{1,0:T(8,128)(2,1)S(1)}, bf16[128,5376]{1,0:T(8,128)(2,1)}, u32[]{:S(2)}, u32[]{:S(2)}) collective-permute-start(bf16[128,5376]{1,0:T(8,128)(2,1)S(1)} %bitcast.50), channel_id=1, source_target_pairs={{0,32},{16,112},{32,64},{48,16},{64,96},{80,48},{96,0},{112,80},{1... | collective-permute-start | bytes 4128776 | tf_op jit(solution)/shard_map/ppermute | solution.py:35
  47.6 28.8 %copy-start.1 = (bf16[128,5376]{1,0:T(8,128)(2,1)}, bf16[128,5376]{1,0:T(8,128)(2,1)S(1)}, u32[]{:S(2)}) copy-start(bf16[128,5376]{1,0:T(8,128)(2,1)S(1)} %collective-permute-done.6.refs_5_) | copy-start | bytes 4128772
  76.5 11.8 %copy-start.2 = (bf16[128,5376]{1,0:T(8,128)(2,1)}, bf16[128,5376]{1,0:T(8,128)(2,1)S(1)}, u32[]{:S(2)}) copy-start(bf16[128,5376]{1,0:T(8,128)(2,1)S(1)} %collective-permute-done.5.refs_4_) | copy-start | bytes 4128772
  76.8 11.7 %collective-permute-start.11 = (bf16[128,5376]{1,0:T(8,128)(2,1)}, bf16[128,5376]{1,0:T(8,128)(2,1)}, u32[]{:S(2)}, u32[]{:S(2)}) collective-permute-start(bf16[128,5376]{1,0:T(8,128)(2,1)} %collective-permute-done.4.refs_3_), channel_id=1, source_target_pairs={{0,16},{16,0},{1,17},{17,1},{2,18},{18,2},{3,19},{19,3},{4,20},{20... | collective-permute-start | bytes 4128776 | tf_op jit(solution)/shard_map/ppermute | solution.py:26
  78.8 57.1 %collective-permute-start.10 = (bf16[128,7168]{1,0:T(8,128)(2,1)}, bf16[128,7168]{1,0:T(8,128)(2,1)}, u32[]{:S(2)}, u32[]{:S(2)}) collective-permute-start(bf16[128,7168]{1,0:T(8,128)(2,1)} %bitcast.18.refs_0_.refs_7_), channel_id=1, source_target_pairs={{0,16},{16,0},{1,17},{17,1},{2,18},{18,2},{3,19},{19,3},{4,20},{20... | collective-permute-start | bytes 5505032 | tf_op jit(solution)/shard_map/ppermute | solution.py:26
  78.8 57.1 %collective-permute-start.9 = (bf16[128,7168]{1,0:T(8,128)(2,1)}, bf16[128,7168]{1,0:T(8,128)(2,1)}, u32[]{:S(2)}, u32[]{:S(2)}) collective-permute-start(bf16[128,7168]{1,0:T(8,128)(2,1)} %bitcast.18.refs_0_.refs_7_), channel_id=1, source_target_pairs={{0,96},{16,48},{32,0},{48,80},{64,32},{80,112},{96,64},{112,16},{1... | collective-permute-start | bytes 5505032 | tf_op jit(solution)/shard_map/ppermute | solution.py:35
  78.8 57.1 %collective-permute-start.8 = (bf16[128,7168]{1,0:T(8,128)(2,1)}, bf16[128,7168]{1,0:T(8,128)(2,1)}, u32[]{:S(2)}, u32[]{:S(2)}) collective-permute-start(bf16[128,7168]{1,0:T(8,128)(2,1)} %bitcast.18.refs_0_.refs_7_), channel_id=1, source_target_pairs={{0,32},{16,112},{32,64},{48,16},{64,96},{80,48},{96,0},{112,80},{1... | collective-permute-start | bytes 5505032 | tf_op jit(solution)/shard_map/ppermute | solution.py:35
  81.5 54.4 %all-to-all-start.2 = ((bf16[16,8,7168]{2,1,0:T(8,128)(2,1)}), bf16[16,8,7168]{2,1,0:T(8,128)(2,1)}, u32[]{:S(2)}, u32[]{:S(2)}) async-start(bf16[16,8,7168]{2,1,0:T(8,128)(2,1)} %pad_maximum_fusion), calls=%async_computation.2 | async-start | bytes 3670016 | tf_op jit(solution)/shard_map/all_to_all | solution.py:30
  88.3 3.3 %collective-permute-start.12 = (bf16[128,5376]{1,0:T(8,128)(2,1)S(1)}, bf16[128,5376]{1,0:T(8,128)(2,1)}, u32[]{:S(2)}, u32[]{:S(2)}) collective-permute-start(bf16[128,5376]{1,0:T(8,128)(2,1)S(1)} %collective-permute-done.5.refs_4_), channel_id=1, source_target_pairs={{0,16},{16,0},{1,17},{17,1},{2,18},{18,2},{3,19},{19,3},{4,20},{20... | collective-permute-start | bytes 4128776 | tf_op jit(solution)/shard_map/ppermute | solution.py:26
  88.5 47.4 %collective-permute-start.7 = (bf16[128,5376]{1,0:T(8,128)(2,1)}, bf16[128,5376]{1,0:T(8,128)(2,1)}, u32[]{:S(2)}, u32[]{:S(2)}) collective-permute-start(bf16[128,5376]{1,0:T(8,128)(2,1)} %collective-permute-done.4.refs_3_), channel_id=1, source_target_pairs={{0,32},{16,112},{32,64},{48,16},{64,96},{80,48},{96,0},{112,80},{1... | collective-permute-start | bytes 4128776 | tf_op jit(solution)/shard_map/ppermute | solution.py:35
  135.9 26.2 %collective-permute-start.15 = (bf16[128,7168]{1,0:T(8,128)(2,1)}, bf16[128,7168]{1,0:T(8,128)(2,1)}, u32[]{:S(2)}, u32[]{:S(2)}) collective-permute-start(bf16[128,7168]{1,0:T(8,128)(2,1)} %collective-permute-done.8.refs_1_.refs_8_), channel_id=1, source_target_pairs={{0,16},{16,0},{1,17},{17,1},{2,18},{18,2},{3,19},{19,3},{4,20},{20... | collective-permute-start | bytes 5505032 | tf_op jit(solution)/shard_map/ppermute | solution.py:26
  137.6 16.6 %collective-permute-start.13 = (bf16[128,7168]{1,0:T(8,128)(2,1)}, bf16[128,7168]{1,0:T(8,128)(2,1)}, u32[]{:S(2)}, u32[]{:S(2)}) collective-permute-start(bf16[128,7168]{1,0:T(8,128)(2,1)} %bitcast.19.refs_2_.refs_3_.refs_4_.refs_8_.refs_10_.refs_11_.refs_12_.refs_16_), channel_id=1, source_target_pairs={{0,16},{16,0},{1,17},{17,1},{2,18},{18,2},{3,19},{19,3},{4,20},{20... | collective-permute-start | bytes 5505032 | tf_op jit(solution)/shard_map/ppermute | solution.py:26
  137.7 24.4 %collective-permute-start.16 = (bf16[128,7168]{1,0:T(8,128)(2,1)}, bf16[128,7168]{1,0:T(8,128)(2,1)}, u32[]{:S(2)}, u32[]{:S(2)}) collective-permute-start(bf16[128,7168]{1,0:T(8,128)(2,1)} %collective-permute-done.9.refs_2_.refs_9_), channel_id=1, source_target_pairs={{0,16},{16,0},{1,17},{17,1},{2,18},{18,2},{3,19},{19,3},{4,20},{20... | collective-permute-start | bytes 5505032 | tf_op jit(solution)/shard_map/ppermute | solution.py:26
  138.1 24.0 %collective-permute-start.17 = (bf16[128,7168]{1,0:T(8,128)(2,1)}, bf16[128,7168]{1,0:T(8,128)(2,1)}, u32[]{:S(2)}, u32[]{:S(2)}) collective-permute-start(bf16[128,7168]{1,0:T(8,128)(2,1)} %collective-permute-done.8.refs_1_.refs_8_), channel_id=1, source_target_pairs={{0,32},{16,112},{32,64},{48,16},{64,96},{80,48},{96,0},{112,80},{1... | collective-permute-start | bytes 5505032 | tf_op jit(solution)/shard_map/ppermute | solution.py:35
  139.4 9.2 %collective-permute-start.14 = (bf16[128,5376]{1,0:T(8,128)(2,1)}, bf16[128,5376]{1,0:T(8,128)(2,1)}, u32[]{:S(2)}, u32[]{:S(2)}) collective-permute-start(bf16[128,5376]{1,0:T(8,128)(2,1)} %collective-permute-done.7.refs_2_.refs_8_), channel_id=1, source_target_pairs={{0,16},{16,0},{1,17},{17,1},{2,18},{18,2},{3,19},{19,3},{4,20},{20... | collective-permute-start | bytes 4128776 | tf_op jit(solution)/shard_map/ppermute | solution.py:26
  162.1 4.6 %collective-permute-start.18 = (bf16[128,7168]{1,0:T(8,128)(2,1)}, bf16[128,7168]{1,0:T(8,128)(2,1)}, u32[]{:S(2)}, u32[]{:S(2)}) collective-permute-start(bf16[128,7168]{1,0:T(8,128)(2,1)} %collective-permute-done.17.refs_13_), channel_id=1, source_target_pairs={{0,16},{16,0},{1,17},{17,1},{2,18},{18,2},{3,19},{19,3},{4,20},{20... | collective-permute-start | bytes 5505032 | tf_op jit(solution)/shard_map/ppermute | solution.py:26
  179.5 21.4 %all-to-all-start.3 = ((f32[128,1,8]{2,1,0:T(1,128)}), f32[128,1,8]{2,1,0:T(1,128)S(1)}, u32[]{:S(2)}, u32[]{:S(2)}) async-start(f32[128,1,8]{2,1,0:T(1,128)} %bitcast.57), calls=%async_computation.3 | async-start | bytes 131072 | tf_op jit(solution)/shard_map/all_to_all | solution.py:295

commit v2 on v1

--- a/solution.py
+++ b/solution.py
@@ -347,14 +347,14 @@
     ties = (x, rounds, dy, row_order())
     order = lax.optimization_barrier(ties)[3]
     on_x, back_x = on(x, *ties), back(x, *ties)
-    other_x = swap(after(x, *ties))
+    other_x, other_on = swap(after(x, *ties)), swap(on_x)
     dy = exchange_yz(after(dy, *ties))
 
-    ties = (dy, on_x, back_x, other_x)
+    ties = (dy, on_x, back_x, other_x, other_on)
     again_x, on_dy, back_dy = on(on_x, *ties), on(dy, *ties), back(dy, *ties)
     rounds = exchange_yz(after(rounds, *ties))
     near_x = lax.optimization_barrier((x, on_x, back_x, *ties))[:3]
-    near_x = (*near_x, other_x, swap(near_x[1]), swap(near_x[2]))
+    near_x = (*near_x, other_x, other_on, swap(near_x[2]))
     other_dy = swap(after(dy, *ties))
     pre = forward(near_x, w_gate, w_up, 0, all_rows)
 

time: 202 us -> 194 us (0.960)
  waiting for transfers between devices: 82 us -> 75.2 us
  starting transfers between devices: 50.3 us -> 47.4 us
    ppermute x10, waiting for transfers between devices: 65.1 us -> 55.8 us  [hop(): return lax.ppermute(x, ('x', 'core'), pairs)]
    ppermute x9, starting transfers between devices: 7.27 us -> 14.4 us  [shift(): return lax.ppermute(x, axis, [(i, (i + by) % n) for i in range(n)])]
    ppermute x10, starting transfers between devices: 15 us -> 11.1 us  [hop(): return lax.ppermute(x, ('x', 'core'), pairs)]
    all_to_all x1, starting transfers between devices: 7.57 us -> 3.78 us  [return_rows(): got = lax.all_to_all(row_gate, ('x', 'core', 'z', 'y'), 0, 0, tiled=True)]
    ppermute x9, waiting for transfers between devices: 7.31 us -> 9.81 us  [shift(): return lax.ppermute(x, axis, [(i, (i + by) % n) for i in range(n)])]
    all_to_all x3, starting transfers between devices: 20.5 us -> 18.1 us  [exchange_yz(): lax.all_to_all(tiles, ('z', 'y'), 0, 0, tiled=True)]
  transfers between devices with their start and end apart: 23 -> 23, of which waited for: 9 -> 8; matrix products, arithmetic and copies ran while one was open for 5% -> 5% of each run, Pallas kernels for 21% -> 22%
where the time goes in v2:
time: 194 us; the launch traced here: 193 us
  waiting for transfers between devices  75.2 us (39%)
  Pallas kernels  55.8 us (29%)
  starting transfers between devices  47.4 us (24%)
  matrix products  7.75 us (4%)
  other arithmetic  3.31 us (2%)
  local copies, waits for them, and re-layouts  2.85 us (1%)
    ppermute x10, waiting for transfers between devices, hop(): return lax.ppermute(x, ('x', 'core'), pairs)  55.8 us
    all_to_all x3, starting transfers between devices, exchange_yz(): lax.all_to_all(tiles, ('z', 'y'), 0, 0, tiled=True)  18.1 us
    pallas_call x2, Pallas kernels, forward(): pl.pallas_call(kernel, grid=(size // block,), in_specs=[pl.BlockSpec((1,...  14.5 us
    ppermute x9, starting transfers between devices, shift(): return lax.ppermute(x, axis, [(i, (i + by) % n) for i in range(n)])  14.4 us
    pallas_call x1, Pallas kernels, up_terms(): pl.pallas_call(kernel, grid=(steps + last_steps,), in_specs=[whole, whole...  13.8 us
    pallas_call x1, Pallas kernels, down_terms(): pl.pallas_call(kernel, grid=(steps,), in_specs=[pl.BlockSpec(memory_space...  12.8 us
    ppermute x10, starting transfers between devices, hop(): return lax.ppermute(x, ('x', 'core'), pairs)  11.1 us
    ppermute x9, waiting for transfers between devices, shift(): return lax.ppermute(x, axis, [(i, (i + by) % n) for i in range(n)])  9.81 us
  transfers between devices with their start and end apart: 23, of which 8 were waited for; matrix products, arithmetic and copies ran while one was open for 5% of the time, Pallas kernels for 22%

profile of v2, /device:TPU:1, one launch (start us, length us, event | category | flops | bytes accessed | tf_op | source)
XLA Modules:
  0.0 193.3 jit_solution(17315174267685670217)
XLA Ops:
  0.7 0.1 eq.66
  0.7 0.8 compare_reduce_fusion
  1.5 0.1 copy.24
  1.7 0.2 reduce_window_sum.11
  2.0 1.4 convolution_convert_fusion.2
  3.3 2.1 %collective-permute-start.1 = (bf16[128,1792]{1,0:T(8,128)(2,1)S(1)}, bf16[128,1792]{1,0:T(8,128)(2,1)S(1)}, u32[]{:S(2)}, u32[]{:S(2)}) collective-permute-start(bf16[128,1792]{1,0:T(8,128)(2,1)S(1)} %convolution_convert_fusion.2), channel_id=1, source_target_pairs={{0,96},{16,48},{32,0},{48,80},{64,32},{80,112},{96,64},{112,16},{1... | collective-permute-start | bytes 1376264 | tf_op jit(solution)/shard_map/ppermute | solution.py:35
  5.5 1.3 collective-permute-start
  6.8 3.0 %fusion.1 = bf16[16,8,5376]{2,1,0:T(8,128)(2,1)} fusion(bf16[128,7168]{1,0:T(8,128)(2,1)} %param.7, s32[128]{0:T(128)S(1)} %eq.66, s32[128,16]{0,1:T(8,128)S(1)} %copy.25, pred[128,16]{0,1:T(8,128)(4,1)S(1)} %copy.26), kind=kOutput, calls=%fused_computation.3 | convolution fusion | flops 176881664 | bytes 2763264 | tf_op jit(solution)/shard_map/dot_general | solution.py:320
  9.8 8.0 %all-to-all-start = ((bf16[16,8,5376]{2,1,0:T(8,128)(2,1)}), bf16[16,8,5376]{2,1,0:T(8,128)(2,1)S(1)}, u32[]{:S(2)}, u32[]{:S(2)}) async-start(bf16[16,8,5376]{2,1,0:T(8,128)(2,1)} %fusion.1), calls=%async_computation | async-start | bytes 2752512 | tf_op jit(solution)/shard_map/all_to_all | solution.py:30
  18.0 0.7 slice.16
  18.7 2.7 %collective-permute-start.2 = (bf16[64,1792]{1,0:T(8,128)(2,1)}, bf16[64,1792]{1,0:T(8,128)(2,1)S(1)}, u32[]{:S(2)}, u32[]{:S(2)}) collective-permute-start(bf16[64,1792]{1,0:T(8,128)(2,1)} %slice.16), channel_id=1, source_target_pairs={{0,32},{16,112},{32,64},{48,16},{64,96},{80,48},{96,0},{112,80},{1... | collective-permute-start | bytes 688136 | tf_op jit(solution)/shard_map/ppermute | solution.py:35
  21.3 0.1 fusion.4
  21.5 0.7 stack.35.refs_0_
  22.2 3.4 %fusion = bf16[16,8,7168]{2,1,0:T(8,128)(2,1)} fusion(bf16[128,7168]{1,0:T(8,128)(2,1)} %param.8, bf16[128,16]{0,1:T(8,128)(2,1)S(1)} %fusion.4, s32[128]{0:T(128)S(1)} %eq.66, s32[128,16]{0,1:T(8,128)S(1)} %copy.25, pred[128,16]{0,1:T(8,128)(4,1)S(1)} %copy.26), kind=kOutput, calls=%fused_computation.1 | convolution fusion | flops 235847680 | bytes 3684864 | tf_op jit(solution)/shard_map/dot_general | solution.py:320
  25.6 0.6 collective-permute-done.2
  26.3 1.4 pad_maximum_fusion
  27.7 9.6 %all-to-all-done = bf16[16,8,5376]{2,1,0:T(8,128)(2,1)S(1)} async-done(((bf16[16,8,5376]{2,1,0:T(8,128)(2,1)}), bf16[16,8,5376]{2,1,0:T(8,128)(2,1)S(1)}, u32[]{:S(2)}, u32[]{:S(2)}) %all-to-all-start) | async-done | bytes 1376288 | tf_op jit(solution)/shard_map/all_to_all | solution.py:30
  37.3 5.7 %all-to-all-start.1 = ((bf16[16,8,7168]{2,1,0:T(8,128)(2,1)}), bf16[16,8,7168]{2,1,0:T(8,128)(2,1)}, u32[]{:S(2)}, u32[]{:S(2)}) async-start(bf16[16,8,7168]{2,1,0:T(8,128)(2,1)} %fusion), calls=%async_computation.1 | async-start | bytes 3670016 | tf_op jit(solution)/shard_map/all_to_all | solution.py:30
  42.9 2.1 %collective-permute-start.6 = (bf16[128,5376]{1,0:T(8,128)(2,1)S(1)}, bf16[128,5376]{1,0:T(8,128)(2,1)S(1)}, u32[]{:S(2)}, u32[]{:S(2)}) collective-permute-start(bf16[128,5376]{1,0:T(8,128)(2,1)S(1)} %bitcast.49), channel_id=1, source_target_pairs={{0,16},{16,0},{1,17},{17,1},{2,18},{18,2},{3,19},{19,3},{4,20},{20... | collective-permute-start | bytes 4128776 | tf_op jit(solution)/shard_map/ppermute | solution.py:26
  45.0 1.2 collective-permute-start.5
  46.2 14.9 %collective-permute-done.4.refs_3_ = bf16[128,5376]{1,0:T(8,128)(2,1)} collective-permute-done((bf16[128,5376]{1,0:T(8,128)(2,1)S(1)}, bf16[128,5376]{1,0:T(8,128)(2,1)}, u32[]{:S(2)}, u32[]{:S(2)}) %collective-permute-start.4) | collective-permute-done | bytes 1376288 | tf_op jit(solution)/shard_map/ppermute | solution.py:35
  61.2 9.2 %collective-permute-start.7 = (bf16[128,5376]{1,0:T(8,128)(2,1)}, bf16[128,5376]{1,0:T(8,128)(2,1)}, u32[]{:S(2)}, u32[]{:S(2)}) collective-permute-start(bf16[128,5376]{1,0:T(8,128)(2,1)} %collective-permute-done.4.refs_3_), channel_id=1, source_target_pairs={{0,16},{16,0},{1,17},{17,1},{2,18},{18,2},{3,19},{19,3},{4,20},{20... | collective-permute-start | bytes 4128776 | tf_op jit(solution)/shard_map/ppermute | solution.py:26
  70.4 1.1 copy-done.1
  71.5 2.5 %collective-permute-done.5.refs_4_ = bf16[128,5376]{1,0:T(8,128)(2,1)S(1)} collective-permute-done((bf16[128,5376]{1,0:T(8,128)(2,1)S(1)}, bf16[128,5376]{1,0:T(8,128)(2,1)S(1)}, u32[]{:S(2)}, u32[]{:S(2)}) %collective-permute-start.5) | collective-permute-done | bytes 1376288 | tf_op jit(solution)/shard_map/ppermute | solution.py:35
  74.0 0.1 collective-permute-start.11
  74.1 2.7 %collective-permute-start.9 = (bf16[128,7168]{1,0:T(8,128)(2,1)}, bf16[128,7168]{1,0:T(8,128)(2,1)}, u32[]{:S(2)}, u32[]{:S(2)}) collective-permute-start(bf16[128,7168]{1,0:T(8,128)(2,1)} %bitcast.18.refs_0_.refs_7_), channel_id=1, source_target_pairs={{0,32},{16,112},{32,64},{48,16},{64,96},{80,48},{96,0},{112,80},{1... | collective-permute-start | bytes 5505032 | tf_op jit(solution)/shard_map/ppermute | solution.py:35
  76.8 4.4 %all-to-all-start.2 = ((bf16[16,8,7168]{2,1,0:T(8,128)(2,1)}), bf16[16,8,7168]{2,1,0:T(8,128)(2,1)}, u32[]{:S(2)}, u32[]{:S(2)}) async-start(bf16[16,8,7168]{2,1,0:T(8,128)(2,1)} %pad_maximum_fusion), calls=%async_computation.2 | async-start | bytes 3670016 | tf_op jit(solution)/shard_map/all_to_all | solution.py:30
  81.3 0.1 collective-permute-start.12
  81.4 0.8 collective-permute-start.8
  82.2 2.4 %collective-permute-done.12.refs_7_ = bf16[128,5376]{1,0:T(8,128)(2,1)} collective-permute-done((bf16[128,5376]{1,0:T(8,128)(2,1)S(1)}, bf16[128,5376]{1,0:T(8,128)(2,1)}, u32[]{:S(2)}, u32[]{:S(2)}) %collective-permute-start.12) | collective-permute-done | bytes 1376288 | tf_op jit(solution)/shard_map/ppermute | solution.py:26
  84.6 9.0 %shard_map.102.refs_4_ = f32[1024,512]{1,0:T(8,128)} custom-call(bf16[1,7168,256]{2,1,0:T(8,128)(2,1)} %refs_0_.5, bf16[1,7168,256]{2,1,0:T(8,128)(2,1)} %refs_1_.6, bf16[128,5376]{1,0:T(8,128)(2,1)} %bitcast.51, bf16[128,5376]{1,0:T(8,128)(2,1)} %collective-permute-done.4.refs_3_, bf16[128,5376]{1,0:T(8,128)(2,1)} %copy-done.2, ...), custom_call_target="tpu_custom_call" | custom-call | flops 1 | bytes 1 | tf_op jit(solution)/shard_map/pallas_call | solution.py:75
  93.6 37.8 %collective-permute-done.8.refs_2_.refs_8_ = bf16[128,5376]{1,0:T(8,128)(2,1)} collective-permute-done((bf16[128,5376]{1,0:T(8,128)(2,1)}, bf16[128,5376]{1,0:T(8,128)(2,1)}, u32[]{:S(2)}, u32[]{:S(2)}) %collective-permute-start.8) | collective-permute-done | bytes 1376288 | tf_op jit(solution)/shard_map/ppermute | solution.py:35
  131.3 1.6 collective-permute-start.15
  132.9 0.1 collective-permute-start.13
  133.0 0.4 collective-permute-start.16
  133.4 0.1 collective-permute-start.17
  133.6 6.7 %shard_map.105.refs_6_ = f32[512,256]{1,0:T(8,128)} custom-call(bf16[1,256,7168]{2,1,0:T(8,128)(2,1)} %refs_1_.7, bf16[128,7168]{1,0:T(8,128)(2,1)} %bitcast.18.refs_0_.refs_7_, bf16[128,7168]{1,0:T(8,128)(2,1)} %collective-permute-done.9.refs_1_.refs_8_, bf16[128,7168]{1,0:T(8,128)(2,1)} %collective-permute-done.10.refs_2_.refs_9_, ...), custom_call_target="tpu_custom_call" | custom-call | flops 1 | bytes 1 | tf_op jit(solution)/shard_map/pallas_call | solution.py:163
  140.3 3.6 %collective-permute-done.14.refs_3_.refs_9_ = bf16[128,5376]{1,0:T(8,128)(2,1)} collective-permute-done((bf16[128,5376]{1,0:T(8,128)(2,1)}, bf16[128,5376]{1,0:T(8,128)(2,1)}, u32[]{:S(2)}, u32[]{:S(2)}) %collective-permute-start.14) | collective-permute-done | bytes 1376288 | tf_op jit(solution)/shard_map/ppermute | solution.py:26
  143.9 5.6 %shard_map.103.refs_10_ = f32[1024,512]{1,0:T(8,128)} custom-call(bf16[1,7168,256]{2,1,0:T(8,128)(2,1)} %refs_0_.5, bf16[1,7168,256]{2,1,0:T(8,128)(2,1)} %refs_1_.6, bf16[128,5376]{1,0:T(8,128)(2,1)} %collective-permute-done.8.refs_2_.refs_8_, bf16[128,5376]{1,0:T(8,128)(2,1)} %collective-permute-done.14.refs_3_.refs_9_, ...), custom_call_target="tpu_custom_call", output_to_operand_aliasing={{}: (4, {})} | custom-call | flops 1 | bytes 1 | tf_op jit(solution)/shard_map/pallas_call | solution.py:75
  149.5 7.9 %shard_map.104 = (f32[1024,256]{1,0:T(8,128)}, f32[1024,256]{1,0:T(8,128)}, bf16[1024,256]{1,0:T(8,128)(2,1)}, bf16[256,1024]{1,0:T(8,128)(2,1)}) custom-call(bf16[1,7168,256]{2,1,0:T(8,128)(2,1)} %refs_0_.5, bf16[1,7168,256]{2,1,0:T(8,128)(2,1)} %refs_1_.6, bf16[128,7168]{1,0:T(8,128)(2,1)} %bitcast.19.refs_2_.refs_3_.refs_4_.refs_8_.refs_10_.refs_11_.refs_12_.refs_16_, ...), custom_call_target="tpu_custom_call" | custom-call | flops 1 | bytes 1 | tf_op jit(solution)/shard_map/pallas_call | solution.py:127
  157.5 0.8 collective-permute-start.18
  158.3 3.8 %collective-permute-done.18.refs_14_ = bf16[128,7168]{1,0:T(8,128)(2,1)} collective-permute-done((bf16[128,7168]{1,0:T(8,128)(2,1)}, bf16[128,7168]{1,0:T(8,128)(2,1)}, u32[]{:S(2)}, u32[]{:S(2)}) %collective-permute-start.18) | collective-permute-done | bytes 1835040 | tf_op jit(solution)/shard_map/ppermute | solution.py:26
  162.0 12.8 %shard_map.106 = (bf16[1,256,7168]{2,1,0:T(8,128)(2,1)}, bf16[1024,256]{1,0:T(8,128)(2,1)}, bf16[1024,256]{1,0:T(8,128)(2,1)}, f32[128,8]{1,0:T(8,128)}) custom-call(s32[8]{0:T(128)} %stack.35.refs_0_, bf16[1,256,7168]{2,1,0:T(8,128)(2,1)} %refs_1_.7, bf16[256,1024]{1,0:T(8,128)(2,1)} %get-tuple-element.43.refs_2_, f32[1024,256]{1,0:T(8,128)} %get-tuple-element.44.refs_3_, ...), custom_call_target="tpu_custom_call" | custom-call | flops 1 | bytes 1 | tf_op jit(solution)/shard_map/pallas_call | solution.py:232
  174.9 3.8 %all-to-all-start.3 = ((f32[128,1,8]{2,1,0:T(1,128)}), f32[128,1,8]{2,1,0:T(1,128)S(1)}, u32[]{:S(2)}, u32[]{:S(2)}) async-start(f32[128,1,8]{2,1,0:T(1,128)} %bitcast.57), calls=%async_computation.3 | async-start | bytes 131072 | tf_op jit(solution)/shard_map/all_to_all | solution.py:295
  178.6 13.8 %shard_map.107 = (bf16[1,7168,256]{2,1,0:T(8,128)(2,1)}, bf16[1,7168,256]{2,1,0:T(8,128)(2,1)}) custom-call(bf16[1024,256]{1,0:T(8,128)(2,1)} %get-tuple-element.52.refs_0_, bf16[1024,256]{1,0:T(8,128)(2,1)} %get-tuple-element.53.refs_1_, bf16[128,5376]{1,0:T(8,128)(2,1)} %bitcast.52, bf16[128,5376]{1,0:T(8,128)(2,1)} %collective-permute-done.4.refs_3_, ...), custom_call_target="tpu_custom_call" | custom-call | flops 1 | bytes 1 | tf_op jit(solution)/shard_map/pallas_call | solution.py:275
  192.5 0.1 select_reduce_fusion
  192.6 0.1 fusion.5
  192.7 0.6 convert_divide_fusion
  (38 shorter events, 0.4 us)
Async XLA Ops:
  3.3 14.5 %collective-permute-start.1 = (bf16[128,1792]{1,0:T(8,128)(2,1)S(1)}, bf16[128,1792]{1,0:T(8,128)(2,1)S(1)}, u32[]{:S(2)}, u32[]{:S(2)}) collective-permute-start(bf16[128,1792]{1,0:T(8,128)(2,1)S(1)} %convolution_convert_fusion.2), channel_id=1, source_target_pairs={{0,96},{16,48},{32,0},{48,80},{64,32},{80,112},{96,64},{112,16},{1... | collective-permute-start | bytes 1376264 | tf_op jit(solution)/shard_map/ppermute | solution.py:35
  5.5 12.5 %collective-permute-start = (bf16[128,1792]{1,0:T(8,128)(2,1)S(1)}, bf16[128,1792]{1,0:T(8,128)(2,1)S(1)}, u32[]{:S(2)}, u32[]{:S(2)}) collective-permute-start(bf16[128,1792]{1,0:T(8,128)(2,1)S(1)} %convolution_convert_fusion.2), channel_id=1, source_target_pairs={{0,32},{16,112},{32,64},{48,16},{64,96},{80,48},{96,0},{112,80},{1... | collective-permute-start | bytes 1376264 | tf_op jit(solution)/shard_map/ppermute | solution.py:35
  9.8 8.0 %copy-start.4 = (bf16[128,8]{0,1:T(8,128)(2,1)S(1)}, bf16[128,8]{0,1:T(8,128)(2,1)}, u32[]{:S(2)}) copy-start(bf16[128,8]{0,1:T(8,128)(2,1)} %param.10) | copy-start | bytes 6148
  9.8 11.5 %copy-start.3 = (s32[128,8]{0,1:T(8,128)S(1)}, s32[128,8]{0,1:T(8,128)}, u32[]{:S(2)}) copy-start(s32[128,8]{0,1:T(8,128)} %param.9) | copy-start | bytes 12292
  9.8 27.5 %all-to-all-start = ((bf16[16,8,5376]{2,1,0:T(8,128)(2,1)}), bf16[16,8,5376]{2,1,0:T(8,128)(2,1)S(1)}, u32[]{:S(2)}, u32[]{:S(2)}) async-start(bf16[16,8,5376]{2,1,0:T(8,128)(2,1)} %fusion.1), calls=%async_computation | async-start | bytes 2752512 | tf_op jit(solution)/shard_map/all_to_all | solution.py:30
  17.9 7.7 %collective-permute-start.3 = (bf16[64,1792]{1,0:T(8,128)(2,1)S(1)}, bf16[64,1792]{1,0:T(8,128)(2,1)S(1)}, u32[]{:S(2)}, u32[]{:S(2)}) collective-permute-start(bf16[64,1792]{1,0:T(8,128)(2,1)S(1)} %slice.17), channel_id=1, source_target_pairs={{0,96},{16,48},{32,0},{48,80},{64,32},{80,112},{96,64},{112,16},{1... | collective-permute-start | bytes 688136 | tf_op jit(solution)/shard_map/ppermute | solution.py:35
  18.7 7.6 %collective-permute-start.2 = (bf16[64,1792]{1,0:T(8,128)(2,1)}, bf16[64,1792]{1,0:T(8,128)(2,1)S(1)}, u32[]{:S(2)}, u32[]{:S(2)}) collective-permute-start(bf16[64,1792]{1,0:T(8,128)(2,1)} %slice.16), channel_id=1, source_target_pairs={{0,32},{16,112},{32,64},{48,16},{64,96},{80,48},{96,0},{112,80},{1... | collective-permute-start | bytes 688136 | tf_op jit(solution)/shard_map/ppermute | solution.py:35
  37.3 7.8 %copy-start = (bf16[16,8,5376]{2,1,0:T(8,128)(2,1)}, bf16[16,8,5376]{2,1,0:T(8,128)(2,1)S(1)}, u32[]{:S(2)}) copy-start(bf16[16,8,5376]{2,1,0:T(8,128)(2,1)S(1)} %all-to-all-done) | copy-start | bytes 4128772
  37.3 23.9 %collective-permute-start.4 = (bf16[128,5376]{1,0:T(8,128)(2,1)S(1)}, bf16[128,5376]{1,0:T(8,128)(2,1)}, u32[]{:S(2)}, u32[]{:S(2)}) collective-permute-start(bf16[128,5376]{1,0:T(8,128)(2,1)S(1)} %bitcast.48), channel_id=1, source_target_pairs={{0,32},{16,112},{32,64},{48,16},{64,96},{80,48},{96,0},{112,80},{1... | collective-permute-start | bytes 4128776 | tf_op jit(solution)/shard_map/ppermute | solution.py:35
  37.3 36.7 %all-to-all-start.1 = ((bf16[16,8,7168]{2,1,0:T(8,128)(2,1)}), bf16[16,8,7168]{2,1,0:T(8,128)(2,1)}, u32[]{:S(2)}, u32[]{:S(2)}) async-start(bf16[16,8,7168]{2,1,0:T(8,128)(2,1)} %fusion), calls=%async_computation.1 | async-start | bytes 3670016 | tf_op jit(solution)/shard_map/all_to_all | solution.py:30
  42.9 27.4 %collective-permute-start.6 = (bf16[128,5376]{1,0:T(8,128)(2,1)S(1)}, bf16[128,5376]{1,0:T(8,128)(2,1)S(1)}, u32[]{:S(2)}, u32[]{:S(2)}) collective-permute-start(bf16[128,5376]{1,0:T(8,128)(2,1)S(1)} %bitcast.49), channel_id=1, source_target_pairs={{0,16},{16,0},{1,17},{17,1},{2,18},{18,2},{3,19},{19,3},{4,20},{20... | collective-permute-start | bytes 4128776 | tf_op jit(solution)/shard_map/ppermute | solution.py:26
  45.0 28.9 %collective-permute-start.5 = (bf16[128,5376]{1,0:T(8,128)(2,1)S(1)}, bf16[128,5376]{1,0:T(8,128)(2,1)S(1)}, u32[]{:S(2)}, u32[]{:S(2)}) collective-permute-start(bf16[128,5376]{1,0:T(8,128)(2,1)S(1)} %bitcast.50), channel_id=1, source_target_pairs={{0,96},{16,48},{32,0},{48,80},{64,32},{80,112},{96,64},{112,16},{1... | collective-permute-start | bytes 4128776 | tf_op jit(solution)/shard_map/ppermute | solution.py:35
  61.2 12.8 %collective-permute-start.7 = (bf16[128,5376]{1,0:T(8,128)(2,1)}, bf16[128,5376]{1,0:T(8,128)(2,1)}, u32[]{:S(2)}, u32[]{:S(2)}) collective-permute-start(bf16[128,5376]{1,0:T(8,128)(2,1)} %collective-permute-done.4.refs_3_), channel_id=1, source_target_pairs={{0,16},{16,0},{1,17},{17,1},{2,18},{18,2},{3,19},{19,3},{4,20},{20... | collective-permute-start | bytes 4128776 | tf_op jit(solution)/shard_map/ppermute | solution.py:26
  70.4 1.1 copy-start.1
  74.0 7.3 %copy-start.2 = (bf16[128,5376]{1,0:T(8,128)(2,1)}, bf16[128,5376]{1,0:T(8,128)(2,1)S(1)}, u32[]{:S(2)}) copy-start(bf16[128,5376]{1,0:T(8,128)(2,1)S(1)} %collective-permute-done.5.refs_4_) | copy-start | bytes 4128772
  74.0 57.3 %collective-permute-start.11 = (bf16[128,7168]{1,0:T(8,128)(2,1)}, bf16[128,7168]{1,0:T(8,128)(2,1)}, u32[]{:S(2)}, u32[]{:S(2)}) collective-permute-start(bf16[128,7168]{1,0:T(8,128)(2,1)} %bitcast.18.refs_0_.refs_7_), channel_id=1, source_target_pairs={{0,16},{16,0},{1,17},{17,1},{2,18},{18,2},{3,19},{19,3},{4,20},{20... | collective-permute-start | bytes 5505032 | tf_op jit(solution)/shard_map/ppermute | solution.py:26
  74.1 57.3 %collective-permute-start.10 = (bf16[128,7168]{1,0:T(8,128)(2,1)}, bf16[128,7168]{1,0:T(8,128)(2,1)}, u32[]{:S(2)}, u32[]{:S(2)}) collective-permute-start(bf16[128,7168]{1,0:T(8,128)(2,1)} %bitcast.18.refs_0_.refs_7_), channel_id=1, source_target_pairs={{0,96},{16,48},{32,0},{48,80},{64,32},{80,112},{96,64},{112,16},{1... | collective-permute-start | bytes 5505032 | tf_op jit(solution)/shard_map/ppermute | solution.py:35
  74.1 57.2 %collective-permute-start.9 = (bf16[128,7168]{1,0:T(8,128)(2,1)}, bf16[128,7168]{1,0:T(8,128)(2,1)}, u32[]{:S(2)}, u32[]{:S(2)}) collective-permute-start(bf16[128,7168]{1,0:T(8,128)(2,1)} %bitcast.18.refs_0_.refs_7_), channel_id=1, source_target_pairs={{0,32},{16,112},{32,64},{48,16},{64,96},{80,48},{96,0},{112,80},{1... | collective-permute-start | bytes 5505032 | tf_op jit(solution)/shard_map/ppermute | solution.py:35
  76.8 54.5 %all-to-all-start.2 = ((bf16[16,8,7168]{2,1,0:T(8,128)(2,1)}), bf16[16,8,7168]{2,1,0:T(8,128)(2,1)}, u32[]{:S(2)}, u32[]{:S(2)}) async-start(bf16[16,8,7168]{2,1,0:T(8,128)(2,1)} %pad_maximum_fusion), calls=%async_computation.2 | async-start | bytes 3670016 | tf_op jit(solution)/shard_map/all_to_all | solution.py:30
  81.3 3.3 %collective-permute-start.12 = (bf16[128,5376]{1,0:T(8,128)(2,1)S(1)}, bf16[128,5376]{1,0:T(8,128)(2,1)}, u32[]{:S(2)}, u32[]{:S(2)}) collective-permute-start(bf16[128,5376]{1,0:T(8,128)(2,1)S(1)} %collective-permute-done.5.refs_4_), channel_id=1, source_target_pairs={{0,16},{16,0},{1,17},{17,1},{2,18},{18,2},{3,19},{19,3},{4,20},{20... | collective-permute-start | bytes 4128776 | tf_op jit(solution)/shard_map/ppermute | solution.py:26
  81.4 50.0 %collective-permute-start.8 = (bf16[128,5376]{1,0:T(8,128)(2,1)}, bf16[128,5376]{1,0:T(8,128)(2,1)}, u32[]{:S(2)}, u32[]{:S(2)}) collective-permute-start(bf16[128,5376]{1,0:T(8,128)(2,1)} %collective-permute-done.4.refs_3_), channel_id=1, source_target_pairs={{0,32},{16,112},{32,64},{48,16},{64,96},{80,48},{96,0},{112,80},{1... | collective-permute-start | bytes 4128776 | tf_op jit(solution)/shard_map/ppermute | solution.py:35
  131.3 26.1 %collective-permute-start.15 = (bf16[128,7168]{1,0:T(8,128)(2,1)}, bf16[128,7168]{1,0:T(8,128)(2,1)}, u32[]{:S(2)}, u32[]{:S(2)}) collective-permute-start(bf16[128,7168]{1,0:T(8,128)(2,1)} %collective-permute-done.9.refs_1_.refs_8_), channel_id=1, source_target_pairs={{0,16},{16,0},{1,17},{17,1},{2,18},{18,2},{3,19},{19,3},{4,20},{20... | collective-permute-start | bytes 5505032 | tf_op jit(solution)/shard_map/ppermute | solution.py:26
  132.9 16.5 %collective-permute-start.13 = (bf16[128,7168]{1,0:T(8,128)(2,1)}, bf16[128,7168]{1,0:T(8,128)(2,1)}, u32[]{:S(2)}, u32[]{:S(2)}) collective-permute-start(bf16[128,7168]{1,0:T(8,128)(2,1)} %bitcast.19.refs_2_.refs_3_.refs_4_.refs_8_.refs_10_.refs_11_.refs_12_.refs_16_), channel_id=1, source_target_pairs={{0,16},{16,0},{1,17},{17,1},{2,18},{18,2},{3,19},{19,3},{4,20},{20... | collective-permute-start | bytes 5505032 | tf_op jit(solution)/shard_map/ppermute | solution.py:26
  133.0 24.4 %collective-permute-start.16 = (bf16[128,7168]{1,0:T(8,128)(2,1)}, bf16[128,7168]{1,0:T(8,128)(2,1)}, u32[]{:S(2)}, u32[]{:S(2)}) collective-permute-start(bf16[128,7168]{1,0:T(8,128)(2,1)} %collective-permute-done.10.refs_2_.refs_9_), channel_id=1, source_target_pairs={{0,16},{16,0},{1,17},{17,1},{2,18},{18,2},{3,19},{19,3},{4,20},{20... | collective-permute-start | bytes 5505032 | tf_op jit(solution)/shard_map/ppermute | solution.py:26
  133.4 24.0 %collective-permute-start.17 = (bf16[128,7168]{1,0:T(8,128)(2,1)}, bf16[128,7168]{1,0:T(8,128)(2,1)}, u32[]{:S(2)}, u32[]{:S(2)}) collective-permute-start(bf16[128,7168]{1,0:T(8,128)(2,1)} %collective-permute-done.9.refs_1_.refs_8_), channel_id=1, source_target_pairs={{0,32},{16,112},{32,64},{48,16},{64,96},{80,48},{96,0},{112,80},{1... | collective-permute-start | bytes 5505032 | tf_op jit(solution)/shard_map/ppermute | solution.py:35
  133.6 10.3 %collective-permute-start.14 = (bf16[128,5376]{1,0:T(8,128)(2,1)}, bf16[128,5376]{1,0:T(8,128)(2,1)}, u32[]{:S(2)}, u32[]{:S(2)}) collective-permute-start(bf16[128,5376]{1,0:T(8,128)(2,1)} %collective-permute-done.8.refs_2_.refs_8_), channel_id=1, source_target_pairs={{0,16},{16,0},{1,17},{17,1},{2,18},{18,2},{3,19},{19,3},{4,20},{20... | collective-permute-start | bytes 4128776 | tf_op jit(solution)/shard_map/ppermute | solution.py:26
  157.5 4.6 %collective-permute-start.18 = (bf16[128,7168]{1,0:T(8,128)(2,1)}, bf16[128,7168]{1,0:T(8,128)(2,1)}, u32[]{:S(2)}, u32[]{:S(2)}) collective-permute-start(bf16[128,7168]{1,0:T(8,128)(2,1)} %collective-permute-done.17.refs_13_), channel_id=1, source_target_pairs={{0,16},{16,0},{1,17},{17,1},{2,18},{18,2},{3,19},{19,3},{4,20},{20... | collective-permute-start | bytes 5505032 | tf_op jit(solution)/shard_map/ppermute | solution.py:26
  174.9 17.6 %all-to-all-start.3 = ((f32[128,1,8]{2,1,0:T(1,128)}), f32[128,1,8]{2,1,0:T(1,128)S(1)}, u32[]{:S(2)}, u32[]{:S(2)}) async-start(f32[128,1,8]{2,1,0:T(1,128)} %bitcast.57), calls=%async_computation.3 | async-start | bytes 131072 | tf_op jit(solution)/shard_map/all_to_all | solution.py:295

commit v3 on v2

--- a/solution.py
+++ b/solution.py
@@ -13,7 +13,7 @@
 NX, NC, NZ, NY = 4, 2, 4, 4
 
 X_RAW, X_REST = 1792, 5376
-BLOCK, END_BLOCK = 1792, 896
+BLOCK, END_BLOCK = 1792, 1792
 PARAMS = pltpu.CompilerParams(vmem_limit_bytes=63 * 2**20)
 
 
@@ -262,10 +262,10 @@
 
         def write(row_refs):
             x = joined(row_refs)
-            for pre_ref, out_ref in zip(refs[:2], out_refs):
-                out_ref[0] = lax.dot_general(
-                    x, pre_ref[...], (((0,), (0,)), ((), ())), preferred_element_type=jnp.float32
-                ).astype(jnp.bfloat16)
+            pre = jnp.concatenate([ref[...] for ref in refs[:2]], axis=1)
+            both = lax.dot_general(x, pre, (((0,), (0,)), ((), ())), preferred_element_type=jnp.float32)
+            for k, out_ref in enumerate(out_refs):
+                out_ref[0] = both[:, k * width : (k + 1) * width].astype(jnp.bfloat16)
 
         pl.when(pl.program_id(0) < steps)(lambda: write(refs[2 : 2 + count]))
         pl.when(pl.program_id(0) >= steps)(lambda: write(refs[2 + count : -2]))

time: 194 us -> 194 us (level)
  no operation moved by 1% of the time
where the time goes in v3:
time: 194 us; the launch traced here: 193 us
  waiting for transfers between devices  75.2 us (39%)
  Pallas kernels  55.1 us (28%)
  starting transfers between devices  48.1 us (25%)
  matrix products  7.75 us (4%)
  other arithmetic  3.31 us (2%)
  local copies, waits for them, and re-layouts  2.85 us (1%)
    ppermute x10, waiting for transfers between devices, hop(): return lax.ppermute(x, ('x', 'core'), pairs)  55.8 us
    all_to_all x3, starting transfers between devices, exchange_yz(): lax.all_to_all(tiles, ('z', 'y'), 0, 0, tiled=True)  18.1 us
    ppermute x9, starting transfers between devices, shift(): return lax.ppermute(x, axis, [(i, (i + by) % n) for i in range(n)])  15.1 us
    pallas_call x2, Pallas kernels, forward(): pl.pallas_call(kernel, grid=(size // block,), in_specs=[pl.BlockSpec((1,...  14.5 us
    pallas_call x1, Pallas kernels, up_terms(): pl.pallas_call(kernel, grid=(steps + last_steps,), in_specs=[whole, whole...  13.8 us
    pallas_call x1, Pallas kernels, down_terms(): pl.pallas_call(kernel, grid=(steps,), in_specs=[pl.BlockSpec(memory_space...  12.8 us
    ppermute x10, starting transfers between devices, hop(): return lax.ppermute(x, ('x', 'core'), pairs)  11.1 us
    ppermute x9, waiting for transfers between devices, shift(): return lax.ppermute(x, axis, [(i, (i + by) % n) for i in range(n)])  9.81 us
  transfers between devices with their start and end apart: 23, of which 8 were waited for; matrix products, arithmetic and copies ran while one was open for 5% of the time, Pallas kernels for 22%

profile of v3, /device:TPU:1, one launch (start us, length us, event | category | flops | bytes accessed | tf_op | source)
XLA Modules:
  0.0 193.3 jit_solution(17141311423191585104)
XLA Ops:
  0.7 0.1 eq.66
  0.7 0.8 compare_reduce_fusion
  1.5 0.1 copy.24
  1.7 0.2 reduce_window_sum.11
  2.0 1.4 convolution_convert_fusion.2
  3.3 2.1 %collective-permute-start.1 = (bf16[128,1792]{1,0:T(8,128)(2,1)S(1)}, bf16[128,1792]{1,0:T(8,128)(2,1)S(1)}, u32[]{:S(2)}, u32[]{:S(2)}) collective-permute-start(bf16[128,1792]{1,0:T(8,128)(2,1)S(1)} %convolution_convert_fusion.2), channel_id=1, source_target_pairs={{0,96},{16,48},{32,0},{48,80},{64,32},{80,112},{96,64},{112,16},{1... | collective-permute-start | bytes 1376264 | tf_op jit(solution)/shard_map/ppermute | solution.py:35
  5.5 1.3 collective-permute-start
  6.8 3.0 %fusion.1 = bf16[16,8,5376]{2,1,0:T(8,128)(2,1)} fusion(bf16[128,7168]{1,0:T(8,128)(2,1)} %param.7, s32[128]{0:T(128)S(1)} %eq.66, s32[128,16]{0,1:T(8,128)S(1)} %copy.25, pred[128,16]{0,1:T(8,128)(4,1)S(1)} %copy.26), kind=kOutput, calls=%fused_computation.3 | convolution fusion | flops 176881664 | bytes 2763264 | tf_op jit(solution)/shard_map/dot_general | solution.py:320
  9.8 8.0 %all-to-all-start = ((bf16[16,8,5376]{2,1,0:T(8,128)(2,1)}), bf16[16,8,5376]{2,1,0:T(8,128)(2,1)S(1)}, u32[]{:S(2)}, u32[]{:S(2)}) async-start(bf16[16,8,5376]{2,1,0:T(8,128)(2,1)} %fusion.1), calls=%async_computation | async-start | bytes 2752512 | tf_op jit(solution)/shard_map/all_to_all | solution.py:30
  18.0 0.7 slice.16
  18.7 2.7 %collective-permute-start.2 = (bf16[64,1792]{1,0:T(8,128)(2,1)}, bf16[64,1792]{1,0:T(8,128)(2,1)S(1)}, u32[]{:S(2)}, u32[]{:S(2)}) collective-permute-start(bf16[64,1792]{1,0:T(8,128)(2,1)} %slice.16), channel_id=1, source_target_pairs={{0,32},{16,112},{32,64},{48,16},{64,96},{80,48},{96,0},{112,80},{1... | collective-permute-start | bytes 688136 | tf_op jit(solution)/shard_map/ppermute | solution.py:35
  21.3 0.1 fusion.4
  21.5 0.7 stack.35.refs_0_
  22.2 3.4 %fusion = bf16[16,8,7168]{2,1,0:T(8,128)(2,1)} fusion(bf16[128,7168]{1,0:T(8,128)(2,1)} %param.8, bf16[128,16]{0,1:T(8,128)(2,1)S(1)} %fusion.4, s32[128]{0:T(128)S(1)} %eq.66, s32[128,16]{0,1:T(8,128)S(1)} %copy.25, pred[128,16]{0,1:T(8,128)(4,1)S(1)} %copy.26), kind=kOutput, calls=%fused_computation.1 | convolution fusion | flops 235847680 | bytes 3684864 | tf_op jit(solution)/shard_map/dot_general | solution.py:320
  25.6 0.6 collective-permute-done.2
  26.3 1.4 pad_maximum_fusion
  27.7 9.6 %all-to-all-done = bf16[16,8,5376]{2,1,0:T(8,128)(2,1)S(1)} async-done(((bf16[16,8,5376]{2,1,0:T(8,128)(2,1)}), bf16[16,8,5376]{2,1,0:T(8,128)(2,1)S(1)}, u32[]{:S(2)}, u32[]{:S(2)}) %all-to-all-start) | async-done | bytes 1376288 | tf_op jit(solution)/shard_map/all_to_all | solution.py:30
  37.3 5.7 %all-to-all-start.1 = ((bf16[16,8,7168]{2,1,0:T(8,128)(2,1)}), bf16[16,8,7168]{2,1,0:T(8,128)(2,1)}, u32[]{:S(2)}, u32[]{:S(2)}) async-start(bf16[16,8,7168]{2,1,0:T(8,128)(2,1)} %fusion), calls=%async_computation.1 | async-start | bytes 3670016 | tf_op jit(solution)/shard_map/all_to_all | solution.py:30
  42.9 2.1 %collective-permute-start.6 = (bf16[128,5376]{1,0:T(8,128)(2,1)S(1)}, bf16[128,5376]{1,0:T(8,128)(2,1)S(1)}, u32[]{:S(2)}, u32[]{:S(2)}) collective-permute-start(bf16[128,5376]{1,0:T(8,128)(2,1)S(1)} %bitcast.49), channel_id=1, source_target_pairs={{0,16},{16,0},{1,17},{17,1},{2,18},{18,2},{3,19},{19,3},{4,20},{20... | collective-permute-start | bytes 4128776 | tf_op jit(solution)/shard_map/ppermute | solution.py:26
  45.0 1.2 collective-permute-start.5
  46.2 14.9 %collective-permute-done.4.refs_3_ = bf16[128,5376]{1,0:T(8,128)(2,1)} collective-permute-done((bf16[128,5376]{1,0:T(8,128)(2,1)S(1)}, bf16[128,5376]{1,0:T(8,128)(2,1)}, u32[]{:S(2)}, u32[]{:S(2)}) %collective-permute-start.4) | collective-permute-done | bytes 1376288 | tf_op jit(solution)/shard_map/ppermute | solution.py:35
  61.2 9.2 %collective-permute-start.7 = (bf16[128,5376]{1,0:T(8,128)(2,1)}, bf16[128,5376]{1,0:T(8,128)(2,1)}, u32[]{:S(2)}, u32[]{:S(2)}) collective-permute-start(bf16[128,5376]{1,0:T(8,128)(2,1)} %collective-permute-done.4.refs_3_), channel_id=1, source_target_pairs={{0,16},{16,0},{1,17},{17,1},{2,18},{18,2},{3,19},{19,3},{4,20},{20... | collective-permute-start | bytes 4128776 | tf_op jit(solution)/shard_map/ppermute | solution.py:26
  70.4 1.1 copy-done.1
  71.5 2.5 %collective-permute-done.5.refs_4_ = bf16[128,5376]{1,0:T(8,128)(2,1)S(1)} collective-permute-done((bf16[128,5376]{1,0:T(8,128)(2,1)S(1)}, bf16[128,5376]{1,0:T(8,128)(2,1)S(1)}, u32[]{:S(2)}, u32[]{:S(2)}) %collective-permute-start.5) | collective-permute-done | bytes 1376288 | tf_op jit(solution)/shard_map/ppermute | solution.py:35
  74.0 0.1 collective-permute-start.11
  74.1 2.7 %collective-permute-start.9 = (bf16[128,7168]{1,0:T(8,128)(2,1)}, bf16[128,7168]{1,0:T(8,128)(2,1)}, u32[]{:S(2)}, u32[]{:S(2)}) collective-permute-start(bf16[128,7168]{1,0:T(8,128)(2,1)} %bitcast.18.refs_0_.refs_7_), channel_id=1, source_target_pairs={{0,32},{16,112},{32,64},{48,16},{64,96},{80,48},{96,0},{112,80},{1... | collective-permute-start | bytes 5505032 | tf_op jit(solution)/shard_map/ppermute | solution.py:35
  76.8 4.4 %all-to-all-start.2 = ((bf16[16,8,7168]{2,1,0:T(8,128)(2,1)}), bf16[16,8,7168]{2,1,0:T(8,128)(2,1)}, u32[]{:S(2)}, u32[]{:S(2)}) async-start(bf16[16,8,7168]{2,1,0:T(8,128)(2,1)} %pad_maximum_fusion), calls=%async_computation.2 | async-start | bytes 3670016 | tf_op jit(solution)/shard_map/all_to_all | solution.py:30
  81.3 0.1 collective-permute-start.12
  81.4 0.8 collective-permute-start.8
  82.2 2.4 %collective-permute-done.12.refs_7_ = bf16[128,5376]{1,0:T(8,128)(2,1)} collective-permute-done((bf16[128,5376]{1,0:T(8,128)(2,1)S(1)}, bf16[128,5376]{1,0:T(8,128)(2,1)}, u32[]{:S(2)}, u32[]{:S(2)}) %collective-permute-start.12) | collective-permute-done | bytes 1376288 | tf_op jit(solution)/shard_map/ppermute | solution.py:26
  84.6 9.0 %shard_map.102.refs_4_ = f32[1024,512]{1,0:T(8,128)} custom-call(bf16[1,7168,256]{2,1,0:T(8,128)(2,1)} %refs_0_.5, bf16[1,7168,256]{2,1,0:T(8,128)(2,1)} %refs_1_.6, bf16[128,5376]{1,0:T(8,128)(2,1)} %bitcast.51, bf16[128,5376]{1,0:T(8,128)(2,1)} %collective-permute-done.4.refs_3_, bf16[128,5376]{1,0:T(8,128)(2,1)} %copy-done.2, ...), custom_call_target="tpu_custom_call" | custom-call | flops 1 | bytes 1 | tf_op jit(solution)/shard_map/pallas_call | solution.py:75
  93.6 37.8 %collective-permute-done.8.refs_2_.refs_8_ = bf16[128,5376]{1,0:T(8,128)(2,1)} collective-permute-done((bf16[128,5376]{1,0:T(8,128)(2,1)}, bf16[128,5376]{1,0:T(8,128)(2,1)}, u32[]{:S(2)}, u32[]{:S(2)}) %collective-permute-start.8) | collective-permute-done | bytes 1376288 | tf_op jit(solution)/shard_map/ppermute | solution.py:35
  131.3 1.6 collective-permute-start.15
  132.9 0.1 collective-permute-start.13
  133.0 0.4 collective-permute-start.16
  133.4 0.1 collective-permute-start.17
  133.6 6.7 %shard_map.105.refs_6_ = f32[512,256]{1,0:T(8,128)} custom-call(bf16[1,256,7168]{2,1,0:T(8,128)(2,1)} %refs_1_.7, bf16[128,7168]{1,0:T(8,128)(2,1)} %bitcast.18.refs_0_.refs_7_, bf16[128,7168]{1,0:T(8,128)(2,1)} %collective-permute-done.9.refs_1_.refs_8_, bf16[128,7168]{1,0:T(8,128)(2,1)} %collective-permute-done.10.refs_2_.refs_9_, ...), custom_call_target="tpu_custom_call" | custom-call | flops 1 | bytes 1 | tf_op jit(solution)/shard_map/pallas_call | solution.py:163
  140.3 3.6 %collective-permute-done.14.refs_3_.refs_9_ = bf16[128,5376]{1,0:T(8,128)(2,1)} collective-permute-done((bf16[128,5376]{1,0:T(8,128)(2,1)}, bf16[128,5376]{1,0:T(8,128)(2,1)}, u32[]{:S(2)}, u32[]{:S(2)}) %collective-permute-start.14) | collective-permute-done | bytes 1376288 | tf_op jit(solution)/shard_map/ppermute | solution.py:26
  143.9 5.6 %shard_map.103.refs_10_ = f32[1024,512]{1,0:T(8,128)} custom-call(bf16[1,7168,256]{2,1,0:T(8,128)(2,1)} %refs_0_.5, bf16[1,7168,256]{2,1,0:T(8,128)(2,1)} %refs_1_.6, bf16[128,5376]{1,0:T(8,128)(2,1)} %collective-permute-done.8.refs_2_.refs_8_, bf16[128,5376]{1,0:T(8,128)(2,1)} %collective-permute-done.14.refs_3_.refs_9_, ...), custom_call_target="tpu_custom_call", output_to_operand_aliasing={{}: (4, {})} | custom-call | flops 1 | bytes 1 | tf_op jit(solution)/shard_map/pallas_call | solution.py:75
  149.5 7.2 %shard_map.104 = (f32[1024,256]{1,0:T(8,128)}, f32[1024,256]{1,0:T(8,128)}, bf16[1024,256]{1,0:T(8,128)(2,1)}, bf16[256,1024]{1,0:T(8,128)(2,1)}) custom-call(bf16[1,7168,256]{2,1,0:T(8,128)(2,1)} %refs_0_.5, bf16[1,7168,256]{2,1,0:T(8,128)(2,1)} %refs_1_.6, bf16[128,7168]{1,0:T(8,128)(2,1)} %bitcast.19.refs_2_.refs_3_.refs_4_.refs_8_.refs_10_.refs_11_.refs_12_.refs_16_, ...), custom_call_target="tpu_custom_call" | custom-call | flops 1 | bytes 1 | tf_op jit(solution)/shard_map/pallas_call | solution.py:127
  156.7 1.5 collective-permute-start.18
  158.3 3.8 %collective-permute-done.18.refs_14_ = bf16[128,7168]{1,0:T(8,128)(2,1)} collective-permute-done((bf16[128,7168]{1,0:T(8,128)(2,1)}, bf16[128,7168]{1,0:T(8,128)(2,1)}, u32[]{:S(2)}, u32[]{:S(2)}) %collective-permute-start.18) | collective-permute-done | bytes 1835040 | tf_op jit(solution)/shard_map/ppermute | solution.py:26
  162.0 12.8 %shard_map.106 = (bf16[1,256,7168]{2,1,0:T(8,128)(2,1)}, bf16[1024,256]{1,0:T(8,128)(2,1)}, bf16[1024,256]{1,0:T(8,128)(2,1)}, f32[128,8]{1,0:T(8,128)}) custom-call(s32[8]{0:T(128)} %stack.35.refs_0_, bf16[1,256,7168]{2,1,0:T(8,128)(2,1)} %refs_1_.7, bf16[256,1024]{1,0:T(8,128)(2,1)} %get-tuple-element.43.refs_2_, f32[1024,256]{1,0:T(8,128)} %get-tuple-element.44.refs_3_, ...), custom_call_target="tpu_custom_call" | custom-call | flops 1 | bytes 1 | tf_op jit(solution)/shard_map/pallas_call | solution.py:232
  174.9 3.8 %all-to-all-start.3 = ((f32[128,1,8]{2,1,0:T(1,128)}), f32[128,1,8]{2,1,0:T(1,128)S(1)}, u32[]{:S(2)}, u32[]{:S(2)}) async-start(f32[128,1,8]{2,1,0:T(1,128)} %bitcast.57), calls=%async_computation.3 | async-start | bytes 131072 | tf_op jit(solution)/shard_map/all_to_all | solution.py:295
  178.6 13.8 %shard_map.107 = (bf16[1,7168,256]{2,1,0:T(8,128)(2,1)}, bf16[1,7168,256]{2,1,0:T(8,128)(2,1)}) custom-call(bf16[1024,256]{1,0:T(8,128)(2,1)} %get-tuple-element.52.refs_0_, bf16[1024,256]{1,0:T(8,128)(2,1)} %get-tuple-element.53.refs_1_, bf16[128,5376]{1,0:T(8,128)(2,1)} %bitcast.52, bf16[128,5376]{1,0:T(8,128)(2,1)} %collective-permute-done.4.refs_3_, ...), custom_call_target="tpu_custom_call" | custom-call | flops 1 | bytes 1 | tf_op jit(solution)/shard_map/pallas_call | solution.py:275
  192.5 0.1 select_reduce_fusion
  192.6 0.1 fusion.5
  192.7 0.6 convert_divide_fusion
  (38 shorter events, 0.4 us)
Async XLA Ops:
  3.3 14.5 %collective-permute-start.1 = (bf16[128,1792]{1,0:T(8,128)(2,1)S(1)}, bf16[128,1792]{1,0:T(8,128)(2,1)S(1)}, u32[]{:S(2)}, u32[]{:S(2)}) collective-permute-start(bf16[128,1792]{1,0:T(8,128)(2,1)S(1)} %convolution_convert_fusion.2), channel_id=1, source_target_pairs={{0,96},{16,48},{32,0},{48,80},{64,32},{80,112},{96,64},{112,16},{1... | collective-permute-start | bytes 1376264 | tf_op jit(solution)/shard_map/ppermute | solution.py:35
  5.5 12.5 %collective-permute-start = (bf16[128,1792]{1,0:T(8,128)(2,1)S(1)}, bf16[128,1792]{1,0:T(8,128)(2,1)S(1)}, u32[]{:S(2)}, u32[]{:S(2)}) collective-permute-start(bf16[128,1792]{1,0:T(8,128)(2,1)S(1)} %convolution_convert_fusion.2), channel_id=1, source_target_pairs={{0,32},{16,112},{32,64},{48,16},{64,96},{80,48},{96,0},{112,80},{1... | collective-permute-start | bytes 1376264 | tf_op jit(solution)/shard_map/ppermute | solution.py:35
  9.8 8.0 %copy-start.4 = (bf16[128,8]{0,1:T(8,128)(2,1)S(1)}, bf16[128,8]{0,1:T(8,128)(2,1)}, u32[]{:S(2)}) copy-start(bf16[128,8]{0,1:T(8,128)(2,1)} %param.10) | copy-start | bytes 6148
  9.8 11.5 %copy-start.3 = (s32[128,8]{0,1:T(8,128)S(1)}, s32[128,8]{0,1:T(8,128)}, u32[]{:S(2)}) copy-start(s32[128,8]{0,1:T(8,128)} %param.9) | copy-start | bytes 12292
  9.8 27.5 %all-to-all-start = ((bf16[16,8,5376]{2,1,0:T(8,128)(2,1)}), bf16[16,8,5376]{2,1,0:T(8,128)(2,1)S(1)}, u32[]{:S(2)}, u32[]{:S(2)}) async-start(bf16[16,8,5376]{2,1,0:T(8,128)(2,1)} %fusion.1), calls=%async_computation | async-start | bytes 2752512 | tf_op jit(solution)/shard_map/all_to_all | solution.py:30
  17.9 7.7 %collective-permute-start.3 = (bf16[64,1792]{1,0:T(8,128)(2,1)S(1)}, bf16[64,1792]{1,0:T(8,128)(2,1)S(1)}, u32[]{:S(2)}, u32[]{:S(2)}) collective-permute-start(bf16[64,1792]{1,0:T(8,128)(2,1)S(1)} %slice.17), channel_id=1, source_target_pairs={{0,96},{16,48},{32,0},{48,80},{64,32},{80,112},{96,64},{112,16},{1... | collective-permute-start | bytes 688136 | tf_op jit(solution)/shard_map/ppermute | solution.py:35
  18.7 7.6 %collective-permute-start.2 = (bf16[64,1792]{1,0:T(8,128)(2,1)}, bf16[64,1792]{1,0:T(8,128)(2,1)S(1)}, u32[]{:S(2)}, u32[]{:S(2)}) collective-permute-start(bf16[64,1792]{1,0:T(8,128)(2,1)} %slice.16), channel_id=1, source_target_pairs={{0,32},{16,112},{32,64},{48,16},{64,96},{80,48},{96,0},{112,80},{1... | collective-permute-start | bytes 688136 | tf_op jit(solution)/shard_map/ppermute | solution.py:35
  37.3 7.8 %copy-start = (bf16[16,8,5376]{2,1,0:T(8,128)(2,1)}, bf16[16,8,5376]{2,1,0:T(8,128)(2,1)S(1)}, u32[]{:S(2)}) copy-start(bf16[16,8,5376]{2,1,0:T(8,128)(2,1)S(1)} %all-to-all-done) | copy-start | bytes 4128772
  37.3 23.9 %collective-permute-start.4 = (bf16[128,5376]{1,0:T(8,128)(2,1)S(1)}, bf16[128,5376]{1,0:T(8,128)(2,1)}, u32[]{:S(2)}, u32[]{:S(2)}) collective-permute-start(bf16[128,5376]{1,0:T(8,128)(2,1)S(1)} %bitcast.48), channel_id=1, source_target_pairs={{0,32},{16,112},{32,64},{48,16},{64,96},{80,48},{96,0},{112,80},{1... | collective-permute-start | bytes 4128776 | tf_op jit(solution)/shard_map/ppermute | solution.py:35
  37.3 36.7 %all-to-all-start.1 = ((bf16[16,8,7168]{2,1,0:T(8,128)(2,1)}), bf16[16,8,7168]{2,1,0:T(8,128)(2,1)}, u32[]{:S(2)}, u32[]{:S(2)}) async-start(bf16[16,8,7168]{2,1,0:T(8,128)(2,1)} %fusion), calls=%async_computation.1 | async-start | bytes 3670016 | tf_op jit(solution)/shard_map/all_to_all | solution.py:30
  42.9 27.4 %collective-permute-start.6 = (bf16[128,5376]{1,0:T(8,128)(2,1)S(1)}, bf16[128,5376]{1,0:T(8,128)(2,1)S(1)}, u32[]{:S(2)}, u32[]{:S(2)}) collective-permute-start(bf16[128,5376]{1,0:T(8,128)(2,1)S(1)} %bitcast.49), channel_id=1, source_target_pairs={{0,16},{16,0},{1,17},{17,1},{2,18},{18,2},{3,19},{19,3},{4,20},{20... | collective-permute-start | bytes 4128776 | tf_op jit(solution)/shard_map/ppermute | solution.py:26
  45.0 28.9 %collective-permute-start.5 = (bf16[128,5376]{1,0:T(8,128)(2,1)S(1)}, bf16[128,5376]{1,0:T(8,128)(2,1)S(1)}, u32[]{:S(2)}, u32[]{:S(2)}) collective-permute-start(bf16[128,5376]{1,0:T(8,128)(2,1)S(1)} %bitcast.50), channel_id=1, source_target_pairs={{0,96},{16,48},{32,0},{48,80},{64,32},{80,112},{96,64},{112,16},{1... | collective-permute-start | bytes 4128776 | tf_op jit(solution)/shard_map/ppermute | solution.py:35
  61.2 12.8 %collective-permute-start.7 = (bf16[128,5376]{1,0:T(8,128)(2,1)}, bf16[128,5376]{1,0:T(8,128)(2,1)}, u32[]{:S(2)}, u32[]{:S(2)}) collective-permute-start(bf16[128,5376]{1,0:T(8,128)(2,1)} %collective-permute-done.4.refs_3_), channel_id=1, source_target_pairs={{0,16},{16,0},{1,17},{17,1},{2,18},{18,2},{3,19},{19,3},{4,20},{20... | collective-permute-start | bytes 4128776 | tf_op jit(solution)/shard_map/ppermute | solution.py:26
  70.4 1.1 copy-start.1
  74.0 7.3 %copy-start.2 = (bf16[128,5376]{1,0:T(8,128)(2,1)}, bf16[128,5376]{1,0:T(8,128)(2,1)S(1)}, u32[]{:S(2)}) copy-start(bf16[128,5376]{1,0:T(8,128)(2,1)S(1)} %collective-permute-done.5.refs_4_) | copy-start | bytes 4128772
  74.0 57.3 %collective-permute-start.11 = (bf16[128,7168]{1,0:T(8,128)(2,1)}, bf16[128,7168]{1,0:T(8,128)(2,1)}, u32[]{:S(2)}, u32[]{:S(2)}) collective-permute-start(bf16[128,7168]{1,0:T(8,128)(2,1)} %bitcast.18.refs_0_.refs_7_), channel_id=1, source_target_pairs={{0,16},{16,0},{1,17},{17,1},{2,18},{18,2},{3,19},{19,3},{4,20},{20... | collective-permute-start | bytes 5505032 | tf_op jit(solution)/shard_map/ppermute | solution.py:26
  74.1 57.3 %collective-permute-start.10 = (bf16[128,7168]{1,0:T(8,128)(2,1)}, bf16[128,7168]{1,0:T(8,128)(2,1)}, u32[]{:S(2)}, u32[]{:S(2)}) collective-permute-start(bf16[128,7168]{1,0:T(8,128)(2,1)} %bitcast.18.refs_0_.refs_7_), channel_id=1, source_target_pairs={{0,96},{16,48},{32,0},{48,80},{64,32},{80,112},{96,64},{112,16},{1... | collective-permute-start | bytes 5505032 | tf_op jit(solution)/shard_map/ppermute | solution.py:35
  74.1 57.2 %collective-permute-start.9 = (bf16[128,7168]{1,0:T(8,128)(2,1)}, bf16[128,7168]{1,0:T(8,128)(2,1)}, u32[]{:S(2)}, u32[]{:S(2)}) collective-permute-start(bf16[128,7168]{1,0:T(8,128)(2,1)} %bitcast.18.refs_0_.refs_7_), channel_id=1, source_target_pairs={{0,32},{16,112},{32,64},{48,16},{64,96},{80,48},{96,0},{112,80},{1... | collective-permute-start | bytes 5505032 | tf_op jit(solution)/shard_map/ppermute | solution.py:35
  76.8 54.5 %all-to-all-start.2 = ((bf16[16,8,7168]{2,1,0:T(8,128)(2,1)}), bf16[16,8,7168]{2,1,0:T(8,128)(2,1)}, u32[]{:S(2)}, u32[]{:S(2)}) async-start(bf16[16,8,7168]{2,1,0:T(8,128)(2,1)} %pad_maximum_fusion), calls=%async_computation.2 | async-start | bytes 3670016 | tf_op jit(solution)/shard_map/all_to_all | solution.py:30
  81.3 3.3 %collective-permute-start.12 = (bf16[128,5376]{1,0:T(8,128)(2,1)S(1)}, bf16[128,5376]{1,0:T(8,128)(2,1)}, u32[]{:S(2)}, u32[]{:S(2)}) collective-permute-start(bf16[128,5376]{1,0:T(8,128)(2,1)S(1)} %collective-permute-done.5.refs_4_), channel_id=1, source_target_pairs={{0,16},{16,0},{1,17},{17,1},{2,18},{18,2},{3,19},{19,3},{4,20},{20... | collective-permute-start | bytes 4128776 | tf_op jit(solution)/shard_map/ppermute | solution.py:26
  81.4 50.0 %collective-permute-start.8 = (bf16[128,5376]{1,0:T(8,128)(2,1)}, bf16[128,5376]{1,0:T(8,128)(2,1)}, u32[]{:S(2)}, u32[]{:S(2)}) collective-permute-start(bf16[128,5376]{1,0:T(8,128)(2,1)} %collective-permute-done.4.refs_3_), channel_id=1, source_target_pairs={{0,32},{16,112},{32,64},{48,16},{64,96},{80,48},{96,0},{112,80},{1... | collective-permute-start | bytes 4128776 | tf_op jit(solution)/shard_map/ppermute | solution.py:35
  131.3 25.4 %collective-permute-start.15 = (bf16[128,7168]{1,0:T(8,128)(2,1)}, bf16[128,7168]{1,0:T(8,128)(2,1)}, u32[]{:S(2)}, u32[]{:S(2)}) collective-permute-start(bf16[128,7168]{1,0:T(8,128)(2,1)} %collective-permute-done.9.refs_1_.refs_8_), channel_id=1, source_target_pairs={{0,16},{16,0},{1,17},{17,1},{2,18},{18,2},{3,19},{19,3},{4,20},{20... | collective-permute-start | bytes 5505032 | tf_op jit(solution)/shard_map/ppermute | solution.py:26
  132.9 16.5 %collective-permute-start.13 = (bf16[128,7168]{1,0:T(8,128)(2,1)}, bf16[128,7168]{1,0:T(8,128)(2,1)}, u32[]{:S(2)}, u32[]{:S(2)}) collective-permute-start(bf16[128,7168]{1,0:T(8,128)(2,1)} %bitcast.19.refs_2_.refs_3_.refs_4_.refs_8_.refs_10_.refs_11_.refs_12_.refs_16_), channel_id=1, source_target_pairs={{0,16},{16,0},{1,17},{17,1},{2,18},{18,2},{3,19},{19,3},{4,20},{20... | collective-permute-start | bytes 5505032 | tf_op jit(solution)/shard_map/ppermute | solution.py:26
  133.0 23.7 %collective-permute-start.16 = (bf16[128,7168]{1,0:T(8,128)(2,1)}, bf16[128,7168]{1,0:T(8,128)(2,1)}, u32[]{:S(2)}, u32[]{:S(2)}) collective-permute-start(bf16[128,7168]{1,0:T(8,128)(2,1)} %collective-permute-done.10.refs_2_.refs_9_), channel_id=1, source_target_pairs={{0,16},{16,0},{1,17},{17,1},{2,18},{18,2},{3,19},{19,3},{4,20},{20... | collective-permute-start | bytes 5505032 | tf_op jit(solution)/shard_map/ppermute | solution.py:26
  133.4 23.3 %collective-permute-start.17 = (bf16[128,7168]{1,0:T(8,128)(2,1)}, bf16[128,7168]{1,0:T(8,128)(2,1)}, u32[]{:S(2)}, u32[]{:S(2)}) collective-permute-start(bf16[128,7168]{1,0:T(8,128)(2,1)} %collective-permute-done.9.refs_1_.refs_8_), channel_id=1, source_target_pairs={{0,32},{16,112},{32,64},{48,16},{64,96},{80,48},{96,0},{112,80},{1... | collective-permute-start | bytes 5505032 | tf_op jit(solution)/shard_map/ppermute | solution.py:35
  133.6 10.3 %collective-permute-start.14 = (bf16[128,5376]{1,0:T(8,128)(2,1)}, bf16[128,5376]{1,0:T(8,128)(2,1)}, u32[]{:S(2)}, u32[]{:S(2)}) collective-permute-start(bf16[128,5376]{1,0:T(8,128)(2,1)} %collective-permute-done.8.refs_2_.refs_8_), channel_id=1, source_target_pairs={{0,16},{16,0},{1,17},{17,1},{2,18},{18,2},{3,19},{19,3},{4,20},{20... | collective-permute-start | bytes 4128776 | tf_op jit(solution)/shard_map/ppermute | solution.py:26
  156.7 5.3 %collective-permute-start.18 = (bf16[128,7168]{1,0:T(8,128)(2,1)}, bf16[128,7168]{1,0:T(8,128)(2,1)}, u32[]{:S(2)}, u32[]{:S(2)}) collective-permute-start(bf16[128,7168]{1,0:T(8,128)(2,1)} %collective-permute-done.17.refs_13_), channel_id=1, source_target_pairs={{0,16},{16,0},{1,17},{17,1},{2,18},{18,2},{3,19},{19,3},{4,20},{20... | collective-permute-start | bytes 5505032 | tf_op jit(solution)/shard_map/ppermute | solution.py:26
  174.9 17.6 %all-to-all-start.3 = ((f32[128,1,8]{2,1,0:T(1,128)}), f32[128,1,8]{2,1,0:T(1,128)S(1)}, u32[]{:S(2)}, u32[]{:S(2)}) async-start(f32[128,1,8]{2,1,0:T(1,128)} %bitcast.57), calls=%async_computation.3 | async-start | bytes 131072 | tf_op jit(solution)/shard_map/all_to_all | solution.py:295
